TPU v7x, 256 devices: a whole 4x4x8 slice. The times are simulated.
256 devices in a mesh: blk: 32 (over x, y, core), inner: 8 (over z).
Axes of the slice: x: 4, y: 4, z: 8, core: 2. Of those that a mesh axis runs over, the one named last changes fastest.
Arguments:
- latents: bfloat16 [393216, 2048], P(('blk', 'inner')), may hold values from -60 to 60
- test_matrix: bfloat16 [2048, 320], replicated, may hold values from -6 to 6
Outputs:
- basis_rows: float32 [393216, 320], P(('blk', 'inner'))
- projection: float32 [320, 2048], replicated
All inputs are finite; a program needn't handle non-finite values.
Results may differ from a plain program's by a relative error of at most 0.00039.
Values sent between devices are 32-bit elements; how exact they have to be, the bound alone decides.
No kernel may reach another device: no remote copies, remote signals or barrier semaphores. Data moves between devices by JAX's collectives and lax.ppermute only.
A program may use at most 64 MiB of HBM per device.

v0:
```python
import jax
import jax.numpy as jnp
from jax import lax
from jax.sharding import PartitionSpec as P


def swapped(value, axis, apart):
    mask = 2**apart
    pairs = [(source, source ^ mask) for source in range(lax.axis_size(axis))]
    return lax.ppermute(value, axis, pairs)


def shards(latents, test_matrix):
    width_count = latents.shape[1]
    row_total = latents.shape[0] * lax.axis_size("blk") * lax.axis_size("inner")
    sketch = jnp.dot(latents, test_matrix, preferred_element_type=jnp.float32)
    gram_local = (
        jnp.dot(
            sketch.T, sketch, preferred_element_type=jnp.float32, precision=lax.Precision.HIGHEST
        )
        / row_total
    )
    sketch_low = sketch.astype(jnp.bfloat16)
    partial_proj = jnp.dot(sketch_low.T, latents, preferred_element_type=jnp.float32)
    out_scale = jnp.sqrt(jnp.float32(width_count)) / row_total
    gram_acc = gram_local
    for bit_index in range(lax.axis_size("inner").bit_length() - 1):
        gram_acc = gram_acc + swapped(gram_acc, "inner", bit_index)
    for bit_index in range(lax.axis_size("blk").bit_length() - 1):
        gram_acc = gram_acc + swapped(gram_acc, "blk", bit_index)
    lower_factor = jnp.linalg.cholesky(gram_acc)
    basis_rows = jax.scipy.linalg.solve_triangular(lower_factor, sketch.T, lower=True).T
    summed_proj = lax.psum(partial_proj, ("blk", "inner"))
    projection = (
        jax.scipy.linalg.solve_triangular(lower_factor, summed_proj, lower=True) * out_scale
    )
    return (basis_rows, projection)


def solution(mesh):
    placed = (P(("blk", "inner"), None), P())
    return jax.shard_map(
        shards,
        mesh=mesh,
        in_specs=placed,
        out_specs=(P(("blk", "inner"), None), P()),
        check_vma=False,
    )
```

profile of v0, /device:TPU:2, one launch (start us, length us, event | category | flops | bytes accessed | tf_op | source)
XLA Modules:
  0.0 410.3 jit_solution(5482812967793019202)
XLA Ops:
  7.2 1.3 copy-done
  8.5 5.2 %fusion.36 = f32[1536,320]{0,1:T(8,128)S(1)} fusion(bf16[1536,2048]{1,0:T(8,128)(2,1)} %param.2, bf16[2048,320]{0,1:T(8,128)(2,1)S(1)} %copy-done), kind=kOutput, calls=%fused_computation.72 | convolution fusion | flops 2013265920 | bytes 9568256 | tf_op jit(solution)/shard_map/dot_general | solution.py:16
  13.7 3.2 convolution_multiply_fusion
  16.9 2.0 collective-permute-start
  18.9 11.2 %collective-permute-done = f32[320,320]{0,1:T(8,128)S(1)} collective-permute-done((f32[320,320]{0,1:T(8,128)S(1)}, f32[320,320]{0,1:T(8,128)S(1)}, u32[]{:S(2)}, u32[]{:S(2)}) %collective-permute-start) | collective-permute-done | bytes 409632 | tf_op jit(solution)/shard_map/ppermute | solution.py:10
  30.2 3.4 collective-permute-start.1
  33.5 21.1 %collective-permute-done.1 = f32[320,320]{0,1:T(8,128)S(1)} collective-permute-done((f32[320,320]{0,1:T(8,128)S(1)}, f32[320,320]{0,1:T(8,128)S(1)}, u32[]{:S(2)}, u32[]{:S(2)}) %collective-permute-start.1) | collective-permute-done | bytes 409632 | tf_op jit(solution)/shard_map/ppermute | solution.py:10
  54.7 6.3 %collective-permute-start.2 = (f32[320,320]{0,1:T(8,128)S(1)}, f32[320,320]{0,1:T(8,128)S(1)}, u32[]{:S(2)}, u32[]{:S(2)}) collective-permute-start(f32[320,320]{0,1:T(8,128)S(1)} %add.64), channel_id=1, source_target_pairs={{0,4},{1,5},{2,6},{3,7},{4,0},{5,1},{6,2},{7,3},{8,12},{9,13},{10,... | collective-permute-start | bytes 1228808 | tf_op jit(solution)/shard_map/ppermute | solution.py:10
  60.9 21.6 %collective-permute-done.2 = f32[320,320]{0,1:T(8,128)S(1)} collective-permute-done((f32[320,320]{0,1:T(8,128)S(1)}, f32[320,320]{0,1:T(8,128)S(1)}, u32[]{:S(2)}, u32[]{:S(2)}) %collective-permute-start.2) | collective-permute-done | bytes 409632 | tf_op jit(solution)/shard_map/ppermute | solution.py:10
  82.7 1.9 collective-permute-done.3
  84.6 1.7 collective-permute-start.4
  86.2 11.7 %collective-permute-done.4 = f32[320,320]{0,1:T(8,128)S(1)} collective-permute-done((f32[320,320]{0,1:T(8,128)S(1)}, f32[320,320]{0,1:T(8,128)S(1)}, u32[]{:S(2)}, u32[]{:S(2)}) %collective-permute-start.4) | collective-permute-done | bytes 409632 | tf_op jit(solution)/shard_map/ppermute | solution.py:10
  98.0 3.3 collective-permute-start.5
  101.3 10.7 %collective-permute-done.5 = f32[320,320]{0,1:T(8,128)S(1)} collective-permute-done((f32[320,320]{0,1:T(8,128)S(1)}, f32[320,320]{0,1:T(8,128)S(1)}, u32[]{:S(2)}, u32[]{:S(2)}) %collective-permute-start.5) | collective-permute-done | bytes 409632 | tf_op jit(solution)/shard_map/ppermute | solution.py:10
  112.7 11.0 %collective-permute-done.6 = f32[320,320]{0,1:T(8,128)S(1)} collective-permute-done((f32[320,320]{0,1:T(8,128)S(1)}, f32[320,320]{0,1:T(8,128)S(1)}, u32[]{:S(2)}, u32[]{:S(2)}) %collective-permute-start.6) | collective-permute-done | bytes 409632 | tf_op jit(solution)/shard_map/ppermute | solution.py:10
  123.6 0.8 add.69
  124.5 2.3 collective-permute-start.7
  126.8 3.8 fusion.8
  130.6 6.4 %collective-permute-done.7 = f32[320,320]{0,1:T(8,128)} collective-permute-done((f32[320,320]{0,1:T(8,128)}, f32[320,320]{0,1:T(8,128)}, u32[]{:S(2)}, u32[]{:S(2)}) %collective-permute-start.7) | collective-permute-done | bytes 409632 | tf_op jit(solution)/shard_map/ppermute | solution.py:10
  137.0 2.0 add.70
  139.0 2.1 copy.5
  141.1 1.2 fusion.12
  143.2 11.7 %cholesky.78 = f32[128,128]{1,0:T(8,128)S(1)} custom-call(f32[128,128]{1,0:T(8,128)S(1)} %cholesky.198), custom_call_target="Cholesky" | custom-call | tf_op jit(solution)/shard_map/jit(cholesky)/cholesky | solution.py:31
  154.9 10.4 %custom-call.26 = f32[1,128,128]{1,2,0:T(8,128)} custom-call(f32[1,128,128]{2,1,0:T(8,128)S(1)} %get-tuple-element.24), custom_call_target="InvertDiagBlocksLowerTriangular" | custom-call | tf_op jit(solution)/shard_map/jit(cholesky)/cholesky | solution.py:31
  165.3 0.8 cholesky.174
  166.2 1.8 constant_dynamic-update-slice_fusion.2
  168.0 1.2 slice_subtract_fusion
  169.8 12.5 %cholesky.164 = f32[128,128]{1,0:T(8,128)S(1)} custom-call(f32[128,128]{1,0:T(8,128)} %cholesky.202), custom_call_target="Cholesky" | custom-call | tf_op jit(solution)/shard_map/jit(cholesky)/cholesky | solution.py:31
  183.0 10.8 %custom-call.27 = f32[1,128,128]{1,2,0:T(8,128)S(1)} custom-call(f32[1,128,128]{2,1,0:T(8,128)} %get-tuple-element.21), custom_call_target="InvertDiagBlocksLowerTriangular" | custom-call | tf_op jit(solution)/shard_map/jit(cholesky)/cholesky | solution.py:31
  194.6 1.1 slice_subtract_fusion.1
  195.7 5.8 %cholesky.186 = f32[64,64]{1,0:T(8,128)S(1)} custom-call(f32[64,64]{1,0:T(8,128)S(1)} %slice_subtract_fusion.1), custom_call_target="Cholesky" | custom-call | tf_op jit(solution)/shard_map/jit(cholesky)/cholesky | solution.py:31
  205.4 1.1 select_select_fusion
  207.3 6.9 %while.1 = (s32[]{:T(128)}, f32[320,320]{1,0:T(8,128)}, s32[2,2]{1,0:T(2,128)S(1)}, f32[2,128,128]{2,1,0:T(8,128)}, s32[]{:T(128)}) while((s32[]{:T(128)}, f32[320,320]{1,0:T(8,128)}, s32[2,2]{1,0:T(2,128)S(1)}, f32[2,128,128]{2,1,0:T(8,128)}, s32[]{:T(128)}) %tuple.34), condition=%wide.while_cond, body=%wide.while_body.sunk | while | flops 2 | bytes 132205 | solution.py:32
  207.9 2.8 bitcast_dynamic-update-slice_fusion.2
  211.3 2.8 bitcast_dynamic-update-slice_fusion.2
  214.2 1.6 pad_maximum_fusion
  215.8 30.3 %custom-call.28 = f32[3,128,128]{1,2,0:T(8,128)S(1)} custom-call(f32[3,128,128]{2,1,0:T(8,128)} %pad_maximum_fusion), custom_call_target="InvertDiagBlocksLowerTriangular" | custom-call | tf_op jit(solution)/shard_map/jit(_solve_triangular)/triangular_solve | solution.py:32
  246.1 0.8 fusion.10
  247.0 1.6 convolution_subtract_fusion
  248.6 0.8 fusion.25
  249.4 1.9 convolution_subtract_fusion.2
  251.9 1.4 maximum_bitcast_fusion
  253.3 139.3 %all-reduce.5.cloned.1.call-done = f32[320,2048]{1,0:T(8,128)} async-done(((f32[320,2048]{1,0:T(8,128)}), f32[320,2048]{1,0:T(8,128)}) %all-reduce.5.cloned.1.call-update) | async-done | bytes 2621456 | tf_op jit(solution)/shard_map/psum | solution.py:33
  392.6 2.3 fusion.6
  394.9 2.3 convolution_subtract_fusion.1
  397.1 1.1 fusion.24
  398.2 2.5 convolution_subtract_fusion.3
  401.3 1.8 maximum_multiply_fusion
  (41 shorter events, 9.2 us)
Async XLA Ops:
  7.2 1.3 copy-start
  7.2 385.4 %all-reduce.5.cloned.1.call-start = ((), (), s32[]{:S(2)}) async-start(), calls=%async_computation | async-start | bytes 5242880 | tf_op jit(solution)/shard_map/psum | solution.py:33
  8.5 118.3 %slice-start = ((s8[6291456]{0:T(1024)(128)(4,1)}), s8[4194304]{0:T(1024)(128)(4,1)S(1)}, s32[]{:S(2)}) async-start(s8[6291456]{0:T(1024)(128)(4,1)} %bitcast.58), calls=%async_computation.1 | async-start | bytes 8388608
  13.7 113.1 %slice-start.1 = ((s8[6291456]{0:T(1024)(128)(4,1)}), s8[2097152]{0:T(1024)(128)(4,1)S(1)}, s32[]{:S(2)}) async-start(s8[6291456]{0:T(1024)(128)(4,1)} %bitcast.58), calls=%async_computation.2 | async-start | bytes 4194304
  16.9 13.2 %collective-permute-start = (f32[320,320]{0,1:T(8,128)S(1)}, f32[320,320]{0,1:T(8,128)S(1)}, u32[]{:S(2)}, u32[]{:S(2)}) collective-permute-start(f32[320,320]{0,1:T(8,128)S(1)} %convolution_multiply_fusion), channel_id=1, source_target_pairs={{0,1},{1,0},{2,3},{3,2},{4,5},{5,4},{6,7},{7,6},{8,9},{9,8},{10,11... | collective-permute-start | bytes 1228808 | tf_op jit(solution)/shard_map/ppermute | solution.py:10
  30.2 24.4 %collective-permute-start.1 = (f32[320,320]{0,1:T(8,128)S(1)}, f32[320,320]{0,1:T(8,128)S(1)}, u32[]{:S(2)}, u32[]{:S(2)}) collective-permute-start(f32[320,320]{0,1:T(8,128)S(1)} %add.63), channel_id=1, source_target_pairs={{0,2},{1,3},{2,0},{3,1},{4,6},{5,7},{6,4},{7,5},{8,10},{9,11},{10,... | collective-permute-start | bytes 1228808 | tf_op jit(solution)/shard_map/ppermute | solution.py:10
  54.7 27.8 %collective-permute-start.2 = (f32[320,320]{0,1:T(8,128)S(1)}, f32[320,320]{0,1:T(8,128)S(1)}, u32[]{:S(2)}, u32[]{:S(2)}) collective-permute-start(f32[320,320]{0,1:T(8,128)S(1)} %add.64), channel_id=1, source_target_pairs={{0,4},{1,5},{2,6},{3,7},{4,0},{5,1},{6,2},{7,3},{8,12},{9,13},{10,... | collective-permute-start | bytes 1228808 | tf_op jit(solution)/shard_map/ppermute | solution.py:10
  82.6 2.0 collective-permute-start.3
  84.6 13.3 %collective-permute-start.4 = (f32[320,320]{0,1:T(8,128)S(1)}, f32[320,320]{0,1:T(8,128)S(1)}, u32[]{:S(2)}, u32[]{:S(2)}) collective-permute-start(f32[320,320]{0,1:T(8,128)S(1)} %add.66), channel_id=1, source_target_pairs={{0,16},{8,24},{16,0},{24,8},{32,48},{40,56},{48,32},{56,40},{64,80... | collective-permute-start | bytes 1228808 | tf_op jit(solution)/shard_map/ppermute | solution.py:10
  98.0 14.0 %collective-permute-start.5 = (f32[320,320]{0,1:T(8,128)S(1)}, f32[320,320]{0,1:T(8,128)S(1)}, u32[]{:S(2)}, u32[]{:S(2)}) collective-permute-start(f32[320,320]{0,1:T(8,128)S(1)} %add.67), channel_id=1, source_target_pairs={{0,32},{8,40},{16,48},{24,56},{32,0},{40,8},{48,16},{56,24},{64,96... | collective-permute-start | bytes 1228808 | tf_op jit(solution)/shard_map/ppermute | solution.py:10
  112.0 11.6 %collective-permute-start.6 = (f32[320,320]{0,1:T(8,128)S(1)}, f32[320,320]{0,1:T(8,128)S(1)}, u32[]{:S(2)}, u32[]{:S(2)}) collective-permute-start(f32[320,320]{0,1:T(8,128)S(1)} %add.68), channel_id=1, source_target_pairs={{0,64},{8,72},{16,80},{24,88},{32,96},{40,104},{48,112},{56,120},{... | collective-permute-start | bytes 1228808 | tf_op jit(solution)/shard_map/ppermute | solution.py:10
  124.5 12.6 %collective-permute-start.7 = (f32[320,320]{0,1:T(8,128)}, f32[320,320]{0,1:T(8,128)}, u32[]{:S(2)}, u32[]{:S(2)}) collective-permute-start(f32[320,320]{0,1:T(8,128)} %add.69), channel_id=1, source_target_pairs={{0,128},{8,136},{16,144},{24,152},{32,160},{40,168},{48,176},{56,1... | collective-permute-start | bytes 1228808 | tf_op jit(solution)/shard_map/ppermute | solution.py:10
  142.4 0.8 copy-start.2
  206.5 0.8 copy-start.1
Sparse Core Ops, SparseCore 0:
  130.7 261.8 all-reduce.4
where the time goes:
time: 418 us; the launch traced here: 410 us
  waiting for transfers between devices  235 us (56%)
  other arithmetic  94.7 us (23%)
  matrix products  31.4 us (8%)
  starting transfers between devices  19.7 us (5%)
  between operations  16.5 us (4%)
  local copies, waits for them, and re-layouts  13.2 us (3%)
    psum x1, waiting for transfers between devices, shards(): summed_proj = lax.psum(partial_proj, ('blk', 'inner'))  139 us
    ppermute x8, waiting for transfers between devices, swapped(): return lax.ppermute(value, axis, pairs)  95.5 us
    another operation x10, other arithmetic, shards(): lower_factor = jnp.linalg.cholesky(gram_acc)  54 us
    another operation x7, other arithmetic, shards(): jax.scipy.linalg.solve_triangular(lower_factor, sketch.T, lower=True)  33.1 us
    ppermute x8, starting transfers between devices, swapped(): return lax.ppermute(value, axis, pairs)  19.6 us
    another operation x5, matrix products, shards(): jax.scipy.linalg.solve_triangular(lower_factor, summed_proj, lower=True)  8.67 us
  transfers between devices with their start and end apart: 9, of which 9 were waited for; matrix products, arithmetic and copies ran while one was open for 28% of the time, Pallas kernels for 0%

commit v1 on v0

v1 whole, which is shorter than its diff:
```python
import functools

import jax
import jax.numpy as jnp
from jax import lax
from jax.experimental import pallas as pl
from jax.experimental.pallas import tpu as pltpu
from jax.sharding import PartitionSpec as P

HIGHEST = lax.Precision.HIGHEST
LANES = 128
STEP = 8


def dot(a, b):
    return jnp.dot(a, b, precision=HIGHEST, preferred_element_type=jnp.float32)


def dot_t(a, b):
    return lax.dot_general(
        a, b, (((0,), (0,)), ((), ())), precision=HIGHEST, preferred_element_type=jnp.float32
    )


def reciprocal(d):
    r = pl.reciprocal(d, approx=True)
    r = r * (2.0 - d * r)
    return r * (2.0 - d * r)


def factor_inverse(w, n):
    count = n // 8
    tiles = [w[8 * t : 8 * t + 8, :] for t in range(count)]
    lane = lax.broadcasted_iota(jnp.int32, (8, LANES), 1)
    sub = lax.broadcasted_iota(jnp.int32, (8, LANES), 0)
    pivots = []

    def over_lanes(x, j):
        return jnp.broadcast_to(x[:, j : j + 1], (8, LANES))

    def over_rows(x, i):
        return jnp.broadcast_to(x[i : i + 1, :], (8, LANES))

    for first in range(count):
        j = 8 * first
        cols = [{t: over_lanes(tiles[t], j + k) for t in range(first, count)} for k in range(STEP)]
        group = (lane >= j) & (lane < j + STEP)
        coefs = []
        pivot = jnp.zeros((8, LANES), jnp.float32)
        for k in range(STEP):
            d = over_rows(cols[k][first], k)
            pivot = jnp.where(sub == k, d, pivot)
            inverse = reciprocal(d)
            coef = {t: cols[k][t] * inverse for t in range(first, count)}
            coef[first] = jnp.where(sub > k, coef[first], 0.0)
            coefs.append(coef)
            for m in range(k + 1, STEP):
                value = over_rows(cols[k][first], m)
                for t in range(first, count):
                    cols[m][t] = cols[m][t] - coef[t] * value
        pivots.append(pivot)
        current = jnp.where(group, 0.0, tiles[first])
        rows = []
        for k in range(STEP):
            row = jnp.where(lane == j + k, 1.0, over_rows(current, k))
            rows.append(row)
            current = current - coefs[k][first] * row
        tiles[first] = jnp.where(lane == j + sub, 1.0, current)
        for t in range(first + 1, count):
            x = jnp.where(group, 0.0, tiles[t])
            for k in range(STEP):
                x = x - coefs[k][t] * rows[k]
            tiles[t] = x
    out = []
    for t in range(count):
        out.append(jnp.where(lane <= sub + 8 * t, tiles[t] * lax.rsqrt(pivots[t]), 0.0))
    return jnp.concatenate(out, axis=0)


def chol_kernel(g_ref, m_ref):
    m0 = factor_inverse(g_ref[0:128, 0:128], 128)
    a01 = dot(m0, g_ref[0:128, 128:384])
    m_ref[0:128, 0:128] = m0
    m_ref[0:128, 128:384] = jnp.zeros((128, 256), jnp.float32)
    s11 = g_ref[128:256, 128:256] - dot_t(a01[:, 0:128], a01[:, 0:128])
    m1 = factor_inverse(s11, 128)
    s12 = g_ref[128:256, 256:384] - dot_t(a01[:, 0:128], a01[:, 128:256])
    s22 = g_ref[256:384, 256:384] - dot_t(a01[:, 128:256], a01[:, 128:256])
    b0 = -dot_t(a01, m0)
    a12 = dot(m1, s12)
    s22 = s22 - dot_t(a12, a12)
    m2 = factor_inverse(s22[0:64], 64)
    b10 = dot(m1, b0[0:128])
    m_ref[128:256, 0:128] = b10
    m_ref[128:256, 128:256] = m1
    m_ref[128:256, 256:384] = jnp.zeros((128, 128), jnp.float32)
    b20 = b0[128:192] - dot_t(a12, b10)[0:64]
    b21 = -dot_t(a12, m1)[0:64]
    m_ref[256:320, 0:128] = dot(m2[:, 0:64], b20)
    m_ref[256:320, 128:256] = dot(m2[:, 0:64], b21)
    m_ref[256:320, 256:384] = m2


def chol_inverse(gram):
    return pl.pallas_call(
        chol_kernel,
        out_shape=jax.ShapeDtypeStruct((320, 384), jnp.float32),
        in_specs=[pl.BlockSpec(memory_space=pltpu.VMEM)],
        out_specs=pl.BlockSpec(memory_space=pltpu.VMEM),
        compiler_params=pltpu.CompilerParams(vmem_limit_bytes=32 * 2**20),
        cost_estimate=pl.CostEstimate(flops=10**9, bytes_accessed=10**6, transcendentals=0),
        name="chol_inverse",
    )(gram)


def all_reduced(parts, mine):
    rows = parts.shape[2]
    swap = [(i, i ^ 1) for i in range(lax.axis_size("blk"))]
    chips = lax.axis_size("blk") // 2
    groups = [[2 * i + core for i in range(chips)] for core in range(2)]
    depth = lax.axis_size("inner")

    def exchanged(value):
        return lax.all_to_all(value, "blk", 0, 0, axis_index_groups=groups)

    keep = lax.dynamic_index_in_dim(parts, mine, 0, keepdims=False)
    give = lax.dynamic_index_in_dim(parts, 1 - mine, 0, keepdims=False)
    half = keep + lax.ppermute(give, "blk", swap)
    chunk = exchanged(half).sum(0)
    shares = chunk.reshape(depth, rows // depth, LANES)
    share = lax.all_to_all(shares, "inner", 0, 0).sum(0)
    copies = jnp.broadcast_to(share[None], shares.shape)
    chunk = lax.all_to_all(copies, "inner", 0, 0).reshape(rows, LANES)
    half = exchanged(jnp.broadcast_to(chunk[None], half.shape))
    other = lax.ppermute(half, "blk", swap)
    first = jnp.where(mine == 0, half, other)
    second = jnp.where(mine == 0, other, half)
    return jnp.concatenate([first, second], axis=0)


def shards(latents, test_matrix):
    width = latents.shape[1]
    sketch_width = test_matrix.shape[1]
    row_total = latents.shape[0] * lax.axis_size("blk") * lax.axis_size("inner")
    sketch = jnp.dot(latents, test_matrix, preferred_element_type=jnp.float32)
    gram_local = dot_t(sketch, sketch) / row_total
    cross_local = lax.dot_general(
        sketch.astype(jnp.bfloat16),
        latents,
        (((0,), (0,)), ((), ())),
        preferred_element_type=jnp.float32,
    )

    def by_tiles(value, tiles):
        value = jnp.pad(value, ((0, 0), (0, tiles * LANES - value.shape[1])))
        return value.reshape(sketch_width, tiles, LANES).swapaxes(0, 1).reshape(-1, 10, LANES)

    cross_rows = by_tiles(cross_local, width // LANES).reshape(32, 160, LANES)
    gram_rows = by_tiles(gram_local, 3).reshape(32, 30, LANES)
    parts = jnp.concatenate(
        [cross_rows, gram_rows, jnp.zeros((32, 2, LANES), jnp.float32)], axis=1
    )
    mine = lax.axis_index("blk") % 2
    total = all_reduced(parts.reshape(2, 16, 192, LANES), mine)

    def from_tiles(value, tiles):
        value = value.reshape(tiles, sketch_width, LANES).swapaxes(0, 1)
        return value.reshape(sketch_width, tiles * LANES)

    gram = jnp.pad(from_tiles(total[:, 160:190], 3), ((0, 64), (0, 0)))
    cross = from_tiles(total[:, :160], width // LANES)
    inverse = chol_inverse(gram)[:, :sketch_width]
    basis_rows = lax.dot_general(
        sketch,
        inverse,
        (((1,), (1,)), ((), ())),
        precision=HIGHEST,
        preferred_element_type=jnp.float32,
    )
    projection = dot(inverse, cross) * (jnp.sqrt(jnp.float32(width)) / row_total)
    return (basis_rows, projection)


def solution(mesh):
    placed = (P(("blk", "inner"), None), P())
    return jax.shard_map(
        shards,
        mesh=mesh,
        in_specs=placed,
        out_specs=(P(("blk", "inner"), None), P()),
        check_vma=False,
    )
```

time: 418 us -> 162 us (0.39)
  the two profiles are of different devices: /device:TPU:2 before, /device:TPU:1 now
where the time goes in v1:
time: 162 us; the launch traced here: 161 us
  blocking collectives  73.3 us (45%)
  matrix products  23.7 us (15%)
  local copies, waits for them, and re-layouts  22.9 us (14%)
  Pallas kernels  13.3 us (8%)
  other arithmetic  10.6 us (7%)
  starting transfers between devices  9.5 us (6%)
  waiting for transfers between devices  6.76 us (4%)
    all_to_all x2, blocking collectives, exchanged(): return lax.all_to_all(value, 'blk', 0, 0, axis_index_groups=groups)  47.8 us
    all_to_all x1, blocking collectives, all_reduced(): share = lax.all_to_all(shares, 'inner', 0, 0).sum(0)  15.6 us
    pallas_call x1, Pallas kernels, chol_inverse(): pl.pallas_call(chol_kernel, out_shape=jax.ShapeDtypeStruct((320, 384), jn...  13.3 us
    all_to_all x1, blocking collectives, all_reduced(): chunk = lax.all_to_all(copies, 'inner', 0, 0).reshape(rows, LANES)  9.95 us
    ppermute x1, starting transfers between devices, all_reduced(): other = lax.ppermute(half, 'blk', swap)  6.26 us
    dot_general x1, matrix products, dot(): return jnp.dot(a, b, precision=HIGHEST, preferred_element_type=jnp.float32)  5.85 us
    dot_general x1, matrix products, shards(): sketch = jnp.dot(latents, test_matrix, preferred_element_type=jnp.float32)  5.15 us
    unnamed x9, local copies, waits for them, and re-layouts  4.99 us
  transfers between devices with their start and end apart: 2, of which 2 were waited for; matrix products, arithmetic and copies ran while one was open for 0% of the time, Pallas kernels for 0%

profile of v1, /device:TPU:1, one launch (start us, length us, event | category | flops | bytes accessed | tf_op | source)
XLA Modules:
  0.0 160.8 jit_solution(4920952422057706323)
XLA Ops:
  0.6 0.0 copy-start
  0.7 1.3 copy-done
  2.0 0.0 copy-start.3
  2.0 5.2 %fusion.6 = f32[1536,320]{0,1:T(8,128)S(1)} fusion(bf16[1536,2048]{1,0:T(8,128)(2,1)} %param.2, bf16[2048,320]{0,1:T(8,128)(2,1)S(1)} %copy-done), kind=kOutput, calls=%fused_computation.17 | convolution fusion | flops 2013265920 | bytes 9568256 | tf_op jit(solution)/shard_map/dot_general | solution.py:145
  7.1 0.0 copy-done.3
  7.1 3.8 %convolution_bitcast_fusion = f32[40,16,8,128]{3,2,1,0:T(8,128)} fusion(bf16[1536,2048]{1,0:T(8,128)(2,1)S(1)} %copy-done.3, f32[1536,320]{0,1:T(8,128)S(1)} %fusion.6), kind=kOutput, calls=%fused_computation.6 | convolution fusion | flops 2013757440 | bytes 10878976 | tf_op jit(solution)/shard_map/dot_general | solution.py:147
  10.9 4.1 %convolution_multiply_fusion.1 = f32[320,320]{1,0:T(8,128)} fusion(f32[1536,320]{0,1:T(8,128)S(1)} %fusion.6), kind=kOutput, calls=%fused_computation.9 | convolution fusion | flops 1887539200 | bytes 2375680 | tf_op jit(solution)/shard_map/dot_general | solution.py:20
  15.0 3.5 %copy.29 = f32[40,16,8,128]{3,2,0,1:T(8,128)} copy(f32[40,16,8,128]{3,2,1,0:T(8,128)} %convolution_bitcast_fusion) | data formatting | bytes 5242880 | tf_op jit(solution)/shard_map/reshape | solution.py:156
  18.5 2.0 %copy.21 = f32[320,320]{0,1:T(8,128)} copy(f32[320,320]{1,0:T(8,128)} %convolution_multiply_fusion.1) | data formatting | bytes 819200
  20.5 1.9 %pad.8.clone = f32[320,384]{0,1:T(8,128)} pad(f32[320,320]{0,1:T(8,128)} %copy.21, f32[]{:T(128)} %constant.35.clone.1), padding=0_0x0_64 | pad | bytes 901124 | tf_op jit(solution)/shard_map/jit(_pad)/pad | solution.py:155
  22.4 2.1 %copy.17 = f32[3,320,128]{2,1,0:T(8,128)} copy(f32[3,320,128]{1,2,0:T(8,128)} %bitcast.34) | data formatting | bytes 983040 | tf_op jit(solution)/shard_map/transpose | solution.py:156
  24.5 1.9 %concatenate.12 = f32[2,16,30,128]{3,2,1,0:T(8,128)} reshape(f32[3,320,128]{2,1,0:T(8,128)} %copy.17) | data formatting | bytes 983040 | tf_op jit(solution)/shard_map/concatenate | solution.py:160
  26.3 0.1 pad.14.clone
  26.4 2.4 %maximum_maximum_fusion = f32[2,16,192,128]{3,2,1,0:T(8,128)S(1)} fusion(f32[2,16,30,128]{3,2,1,0:T(8,128)} %concatenate.12, f32[2,16,160,128]{3,2,1,0:T(8,128)} %bitcast.32, f32[192]{0:T(256)S(1)} %pad.14.clone), kind=kLoop, calls=%fused_computation | loop fusion | flops 1572864 | bytes 6259456 | tf_op jit(solution)/shard_map/concatenate | solution.py:160
  28.8 0.0 copy-start.1
  28.8 1.7 %copy-done.1 = f32[2,16,192,128]{3,2,1,0:T(8,128)} copy-done((f32[2,16,192,128]{3,2,1,0:T(8,128)}, f32[2,16,192,128]{3,2,1,0:T(8,128)S(1)}, u32[]{:S(2)}) %copy-start.1) | copy-done | bytes 3145752
  30.4 1.3 dynamic-slice_bitcast_fusion
  31.7 3.2 %collective-permute-start = (f32[16,192,128]{2,1,0:T(8,128)}, f32[16,192,128]{2,1,0:T(8,128)}, u32[]{:S(2)}, u32[]{:S(2)}) collective-permute-start(f32[16,192,128]{2,1,0:T(8,128)} %dynamic-slice_bitcast_fusion), channel_id=1, source_target_pairs={{0,8},{8,0},{16,24},{24,16},{32,40},{40,32},{48,56},{56,48},{64,72... | collective-permute-start | bytes 4718600 | tf_op jit(solution)/shard_map/ppermute | solution.py:128
  35.0 3.4 %collective-permute-done = f32[16,192,128]{2,1,0:T(8,128)} collective-permute-done((f32[16,192,128]{2,1,0:T(8,128)}, f32[16,192,128]{2,1,0:T(8,128)}, u32[]{:S(2)}, u32[]{:S(2)}) %collective-permute-start) | collective-permute-done | bytes 1572896 | tf_op jit(solution)/shard_map/ppermute | solution.py:128
  38.4 2.1 %bitcast_add_fusion = f32[16,192,128]{2,1,0:T(8,128)S(1)} fusion(f32[16,192,128]{2,1,0:T(8,128)} %collective-permute-done, f32[2,16,192,128]{3,2,1,0:T(8,128)} %copy-done.1, s32[]{:T(128)S(6)} %select_n.28), kind=kLoop, calls=%fused_computation.7 | loop fusion | flops 393216 | bytes 4718596 | tf_op jit(solution)/shard_map/add | solution.py:128
  40.4 26.5 %all_to_all.20 = f32[16,192,128]{2,1,0:T(8,128)} all-to-all(f32[16,192,128]{2,1,0:T(8,128)S(1)} %bitcast_add_fusion), channel_id=1, replica_groups={{0,16,32,48,64,80,96,112,128,144,160,176,192,208,224,240},{8,24,40,56,7..., dimensions={0} | all-to-all | bytes 3145728 | tf_op jit(solution)/shard_map/all_to_all | solution.py:124
  66.9 1.5 reduce_sum.18
  68.4 15.6 %all_to_all.21 = f32[8,24,128]{2,1,0:T(8,128)S(1)} all-to-all(f32[8,24,128]{2,1,0:T(8,128)S(1)} %bitcast.37), channel_id=1, replica_groups=mesh['blk'=32,'inner'=8] {'inner'}, dimensions={0} | all-to-all | bytes 196608 | tf_op jit(solution)/shard_map/all_to_all | solution.py:131
  84.0 10.0 %all_to_all.22 = f32[8,24,128]{2,1,0:T(8,128)S(1)} all-to-all(f32[8,24,128]{2,1,0:T(8,128)S(1)} %broadcast_in_dim.17), channel_id=1, replica_groups=mesh['blk'=32,'inner'=8] {'inner'}, dimensions={0} | all-to-all | bytes 196608 | tf_op jit(solution)/shard_map/all_to_all | solution.py:133
  94.0 0.1 broadcast_in_dim.19
  94.1 21.2 %all_to_all.23 = f32[16,192,128]{2,1,0:T(8,128)} all-to-all(f32[16,192,128]{2,1,0:T(8,128)S(1)} %broadcast_in_dim.19), channel_id=1, replica_groups={{0,16,32,48,64,80,96,112,128,144,160,176,192,208,224,240},{8,24,40,56,7..., dimensions={0} | all-to-all | bytes 3145728 | tf_op jit(solution)/shard_map/all_to_all | solution.py:124
  115.4 6.3 %collective-permute-start.1 = (f32[16,192,128]{2,1,0:T(8,128)}, f32[16,192,128]{2,1,0:T(8,128)}, u32[]{:S(2)}, u32[]{:S(2)}) collective-permute-start(f32[16,192,128]{2,1,0:T(8,128)} %all_to_all.23), channel_id=1, source_target_pairs={{0,8},{8,0},{16,24},{24,16},{32,40},{40,32},{48,56},{56,48},{64,72... | collective-permute-start | bytes 4718600 | tf_op jit(solution)/shard_map/ppermute | solution.py:135
  121.6 3.4 %collective-permute-done.1 = f32[16,192,128]{2,1,0:T(8,128)} collective-permute-done((f32[16,192,128]{2,1,0:T(8,128)}, f32[16,192,128]{2,1,0:T(8,128)}, u32[]{:S(2)}, u32[]{:S(2)}) %collective-permute-start.1) | collective-permute-done | bytes 1572896 | tf_op jit(solution)/shard_map/ppermute | solution.py:135
  125.0 2.1 %broadcast_select_fusion.1 = (f32[16,192,128]{2,1,0:T(8,128)S(1)}, f32[16,192,128]{2,1,0:T(8,128)S(1)}) fusion(f32[16,192,128]{2,1,0:T(8,128)} %all_to_all.23, f32[16,192,128]{2,1,0:T(8,128)} %collective-permute-done.1, pred[]{:T(512)S(6)} %eq.6), kind=kLoop, calls=%fused_computation.12 | loop fusion | flops 786432 | bytes 6291457 | tf_op jit(solution)/shard_map/jit(_where)/select_n | solution.py:136
  127.1 1.7 %pad_maximum_fusion = f32[32,160,128]{2,1,0:T(8,128)} fusion(f32[16,192,128]{2,1,0:T(8,128)S(1)} %get-tuple-element.3, f32[16,192,128]{2,1,0:T(8,128)S(1)} %get-tuple-element.2), kind=kLoop, calls=%fused_computation.5 | loop fusion | flops 655360 | bytes 5767168 | tf_op jit(solution)/shard_map/concatenate | solution.py:138
  128.8 0.8 pad_maximum_fusion.1
  129.7 1.9 %reshape.36 = f32[3,320,128]{2,1,0:T(8,128)} reshape(f32[32,30,128]{2,1,0:T(8,128)} %pad_maximum_fusion.1) | data formatting | bytes 983040 | tf_op jit(solution)/shard_map/reshape | solution.py:167
  131.5 2.1 %copy.18 = f32[320,3,128]{0,2,1:T(8,128)} copy(f32[320,3,128]{2,0,1:T(8,128)} %bitcast.36) | data formatting | bytes 983040 | tf_op jit(solution)/shard_map/transpose | solution.py:167
  133.6 2.1 %copy.19 = f32[320,384]{1,0:T(8,128)} copy(f32[320,384]{0,1:T(8,128)} %bitcast.35) | data formatting | bytes 983040 | tf_op jit(solution)/shard_map/reshape | solution.py:168
  135.7 1.1 pad.9.g_ref
  136.7 13.3 %chol_inverse.1 = f32[320,384]{1,0:T(8,128)S(1)} custom-call(f32[384,384]{1,0:T(8,128)S(1)} %pad.9.g_ref), custom_call_target="tpu_custom_call" | custom-call | flops 1000000000 | bytes 1000000 | tf_op jit(solution)/shard_map/chol_inverse/pallas_call | solution.py:105
  150.1 0.0 copy-start.2
  150.1 4.9 %fusion.4 = f32[1536,320]{0,1:T(8,128)} fusion(f32[1536,320]{0,1:T(8,128)S(1)} %fusion.6, f32[320,384]{1,0:T(8,128)S(1)} %chol_inverse.1), kind=kOutput, calls=%fused_computation.15 | convolution fusion | flops 1887436800 | bytes 4423680 | tf_op jit(solution)/shard_map/dot_general | solution.py:173
  154.9 0.0 copy-done.2
  154.9 5.8 %convolution_multiply_fusion = f32[320,2048]{1,0:T(8,128)} fusion(f32[16,40,8,128]{3,2,1,0:T(8,128)S(1)} %bitcast.33, f32[320,384]{1,0:T(8,128)S(1)} %chol_inverse.1), kind=kOutput, calls=%fused_computation.1 | convolution fusion | flops 2517237760 | bytes 5734400 | tf_op jit(solution)/shard_map/dot_general | solution.py:16
  (3 shorter events, 0.0 us)
Async XLA Ops:
  0.6 1.3 copy-start
  2.0 5.2 %copy-start.3 = (bf16[1536,2048]{1,0:T(8,128)(2,1)S(1)}, bf16[1536,2048]{1,0:T(8,128)(2,1)}, u32[]{:S(2)}) copy-start(bf16[1536,2048]{1,0:T(8,128)(2,1)} %param.2) | copy-start | bytes 18874372
  28.8 1.7 %copy-start.1 = (f32[2,16,192,128]{3,2,1,0:T(8,128)}, f32[2,16,192,128]{3,2,1,0:T(8,128)S(1)}, u32[]{:S(2)}) copy-start(f32[2,16,192,128]{3,2,1,0:T(8,128)S(1)} %maximum_maximum_fusion) | copy-start | bytes 9437188
  31.7 6.6 %collective-permute-start = (f32[16,192,128]{2,1,0:T(8,128)}, f32[16,192,128]{2,1,0:T(8,128)}, u32[]{:S(2)}, u32[]{:S(2)}) collective-permute-start(f32[16,192,128]{2,1,0:T(8,128)} %dynamic-slice_bitcast_fusion), channel_id=1, source_target_pairs={{0,8},{8,0},{16,24},{24,16},{32,40},{40,32},{48,56},{56,48},{64,72... | collective-permute-start | bytes 4718600 | tf_op jit(solution)/shard_map/ppermute | solution.py:128
  115.4 9.6 %collective-permute-start.1 = (f32[16,192,128]{2,1,0:T(8,128)}, f32[16,192,128]{2,1,0:T(8,128)}, u32[]{:S(2)}, u32[]{:S(2)}) collective-permute-start(f32[16,192,128]{2,1,0:T(8,128)} %all_to_all.23), channel_id=1, source_target_pairs={{0,8},{8,0},{16,24},{24,16},{32,40},{40,32},{48,56},{56,48},{64,72... | collective-permute-start | bytes 4718600 | tf_op jit(solution)/shard_map/ppermute | solution.py:135
  150.1 4.9 %copy-start.2 = (f32[32,160,128]{2,1,0:T(8,128)S(1)}, f32[32,160,128]{2,1,0:T(8,128)}, u32[]{:S(2)}) copy-start(f32[32,160,128]{2,1,0:T(8,128)} %pad_maximum_fusion) | copy-start | bytes 7864324

commit v2 on v0

v2 whole, which is shorter than its diff:
```python
import functools

import jax
import jax.numpy as jnp
from jax import lax
from jax.experimental import pallas as pl
from jax.experimental.pallas import tpu as pltpu
from jax.sharding import PartitionSpec as P

HIGHEST = lax.Precision.HIGHEST
LANES = 128
STEP = 8


def dot(a, b):
    return jnp.dot(a, b, precision=HIGHEST, preferred_element_type=jnp.float32)


def dot_t(a, b):
    return lax.dot_general(
        a, b, (((0,), (0,)), ((), ())), precision=HIGHEST, preferred_element_type=jnp.float32
    )


def factor_inverse(w, n, scratch):
    count = n // 8
    tiles = [w[8 * t : 8 * t + 8, :] for t in range(count)]
    lane = lax.broadcasted_iota(jnp.int32, (8, LANES), 1)
    sub = lax.broadcasted_iota(jnp.int32, (8, LANES), 0)
    pivots = []

    def over_lanes(x, j):
        return jnp.broadcast_to(x[:, j : j + 1], (8, LANES))

    for first in range(count):
        j = STEP * first
        base = 9 * STEP * first
        group = (lane >= j) & (lane < j + STEP)

        def row(i, base=base):
            return jnp.broadcast_to(scratch[base + i : base + i + 1, :], (8, LANES))

        for k in range(STEP):
            scratch[base + 8 * k : base + 8 * k + 8, :] = over_lanes(tiles[first], j + k)
        scratch[base + 64 : base + 72, :] = jnp.where(group, 0.0, tiles[first])
        square = [[row(8 * k + m) for k in range(m + 1)] for m in range(STEP)]
        rows = [row(64 + m) for m in range(STEP)]
        lower = [[None] * STEP for _ in range(STEP)]
        inverse = []
        pivot = square[0][0]
        for k in range(STEP):
            if k:
                pivot = jnp.where(sub == k, square[k][k], pivot)
            inverse.append(1.0 / square[k][k])
            for m in range(k + 1, STEP):
                lower[m][k] = square[m][k] * inverse[k]
            for m in range(k + 1, STEP):
                for i in range(m, STEP):
                    square[i][m] = square[i][m] - square[i][k] * lower[m][k]
            rows[k] = jnp.where(lane == j + k, 1.0, rows[k])
            for m in range(k + 1, STEP):
                rows[m] = rows[m] - lower[m][k] * rows[k]
        pivots.append(pivot)
        done = rows[0]
        for k in range(1, STEP):
            done = jnp.where(sub == k, rows[k], done)
        tiles[first] = done
        scaled = [rows[k] * inverse[k] for k in range(STEP)]
        for t in range(first + 1, count):
            cols = [over_lanes(tiles[t], j + k) for k in range(STEP)]
            x = jnp.where(group, 0.0, tiles[t])
            for k in range(STEP):
                x = x - cols[k] * scaled[k]
                for m in range(k + 1, STEP):
                    cols[m] = cols[m] - cols[k] * lower[m][k]
            tiles[t] = x
    out = []
    for t in range(count):
        out.append(jnp.where(lane <= sub + 8 * t, tiles[t] * lax.rsqrt(pivots[t]), 0.0))
    return jnp.concatenate(out, axis=0)


def bf16_parts(x):
    high = x.astype(jnp.bfloat16)
    return high, (x - high.astype(jnp.float32)).astype(jnp.bfloat16)


def mxu(a, b, dims=((1,), (0,))):
    return lax.dot_general(a, b, (dims, ((), ())), preferred_element_type=jnp.float32)


ROWS_OF = ((1,), (1,))
VMEM = pl.BlockSpec(memory_space=pltpu.VMEM)
SMEM = pl.BlockSpec(memory_space=pltpu.SMEM)
HBM = pl.BlockSpec(memory_space=pltpu.HBM)
CHIPS = 16
DEPTH = 8
BLOCKS = 6


def shape(*dims, dtype=jnp.float32):
    return jax.ShapeDtypeStruct(dims, dtype)


def call(kernel, name, out_shape, in_specs, out_specs, scratch=(), flops=10**6, moved=10**6, mib=24):
    return pl.pallas_call(
        kernel,
        out_shape=out_shape,
        in_specs=in_specs,
        out_specs=out_specs,
        scratch_shapes=list(scratch),
        compiler_params=pltpu.CompilerParams(vmem_limit_bytes=mib * 2**20),
        cost_estimate=pl.CostEstimate(flops=flops, bytes_accessed=moved, transcendentals=0),
        name=name,
    )


def front_kernel(
    row_total, core_ref, lat_hbm, om_hbm, high_ref, mid_ref, keep_ref, give_ref, lat, om_ref, low, sems
):
    rows, width = lat.shape
    tall = om_ref.shape[0]
    block = rows // BLOCKS
    core = core_ref[0]

    def load(i):
        part = pl.ds(pl.multiple_of(i * block, block), block)
        return pltpu.make_async_copy(lat_hbm.at[part], lat.at[part], sems.at[i])

    test = pltpu.make_async_copy(om_hbm, om_ref, sems.at[BLOCKS])
    test.start()
    for i in range(BLOCKS):
        load(i).start()
    test.wait()

    @pl.loop(0, BLOCKS)
    def _(i):
        load(i).wait()
        part = pl.ds(pl.multiple_of(i * block, block), block)
        s = mxu(om_ref[...], lat[part, :], ROWS_OF)
        high, mid = bf16_parts(s)
        high_ref[:, part] = high
        mid_ref[:, part] = mid
        low[:, part] = (s - high.astype(jnp.float32) - mid.astype(jnp.float32)).astype(jnp.bfloat16)

    for ref, which in ((give_ref, 1 - core), (keep_ref, core)):

        @pl.loop(0, width // 512)
        def _(c, ref=ref, which=which):
            at = pl.multiple_of(which * (width // 2) + c * 256, 256)
            out = mxu(high_ref[...], lat[:, pl.ds(at, 256)])
            for k in range(4):
                piece = out[(k % 2) * (tall // 2) : (k % 2 + 1) * (tall // 2)]
                piece = piece[:, (k // 2) * LANES : (k // 2 + 1) * LANES]
                ref[4 * c + k, 0 : tall // 2, :] = piece

    high = high_ref[...]
    mid = mid_ref[...]
    cross_mid = mxu(high, mid, ROWS_OF) + mxu(high, low[...], ROWS_OF)
    gram = mxu(high, high, ROWS_OF) + (cross_mid + cross_mid.T + mxu(mid, mid, ROWS_OF))
    gram = gram * (1.0 / row_total)
    corner = jnp.concatenate([gram[256:320, 256:320], gram[64:128, 64:128]], axis=1)
    zero = jnp.concatenate([gram[0:64, 0:128], corner, gram[0:128, 128:256]], axis=0)
    last = jnp.concatenate([gram[0:128, 256:320], gram[128:256, 256:320]], axis=1)
    one = jnp.concatenate([last, gram[128:256, 128:256]], axis=0)
    own = jnp.where(core == 0, zero, one).reshape(CHIPS, 16, LANES)
    far = jnp.where(core == 0, one, zero).reshape(CHIPS, 16, LANES)
    keep_ref[:, tall // 2 :, :] = own
    give_ref[:, tall // 2 :, :] = far


def front(core, latents, test_t, row_total):
    rows, width = latents.shape
    tall = test_t.shape[0]
    bf16 = jnp.bfloat16
    return call(
        functools.partial(front_kernel, row_total),
        "front",
        [
            shape(tall, rows, dtype=bf16),
            shape(tall, rows, dtype=bf16),
            shape(CHIPS, tall // 2 + 16, LANES),
            shape(CHIPS, tall // 2 + 16, LANES),
        ],
        [SMEM, HBM, HBM],
        [VMEM] * 4,
        [
            pltpu.VMEM((rows, width), bf16),
            pltpu.VMEM((tall, width), bf16),
            pltpu.VMEM((tall, rows), bf16),
            pltpu.SemaphoreType.DMA((BLOCKS + 1,)),
        ],
        flops=6 * 10**9,
        moved=10**7,
        mib=46,
    )(core, latents, test_t)


def sum_copies_kernel(x_ref, out_ref):
    total = x_ref[0]
    for i in range(1, x_ref.shape[0]):
        total = total + x_ref[i]
    for i in range(out_ref.shape[0]):
        out_ref[i] = total


def sum_copies(x, count):
    return call(sum_copies_kernel, "sum_copies", shape(count, *x.shape[1:]), [VMEM], VMEM)(x)


def factor(zero, one, m_ref, scratch):
    left = jnp.concatenate([zero[0:64, 64:128].T, zero[64:128, 64:128]], axis=1)
    g00 = jnp.concatenate([zero[0:64], left], axis=0)
    blank = jnp.zeros((128, 64), jnp.float32)
    g01 = jnp.concatenate([zero[128:256], one[0:128, 0:64], blank], axis=1)
    g12 = jnp.concatenate([one[0:128, 64:128], blank], axis=1)
    g22 = jnp.concatenate([zero[64:128, 0:64], blank[0:64]], axis=1)
    m0 = factor_inverse(g00, 128, scratch)
    a01 = dot(m0, g01)
    m_ref[0:128, 0:128] = m0
    m_ref[0:128, 128:384] = jnp.zeros((128, 256), jnp.float32)
    m1 = factor_inverse(one[128:256] - dot_t(a01[:, 0:128], a01[:, 0:128]), 128, scratch)
    s12 = g12 - dot_t(a01[:, 0:128], a01[:, 128:256])
    s22 = g22 - dot_t(a01[:, 128:256], a01[:, 128:256])[0:64]
    b0 = -dot_t(a01, m0)
    a12 = dot(m1, s12)
    s22 = s22 - dot_t(a12, a12)[0:64]
    m2 = factor_inverse(s22, 64, scratch)
    b10 = dot(m1, b0[0:128])
    m_ref[128:256, 0:128] = b10
    m_ref[128:256, 128:256] = m1
    m_ref[128:256, 256:384] = jnp.zeros((128, 128), jnp.float32)
    b20 = b0[128:192] - dot_t(a12, b10)[0:64]
    b21 = -dot_t(a12, m1)[0:64]
    m_ref[256:320, 0:128] = dot(m2[:, 0:64], b20)
    m_ref[256:320, 128:256] = dot(m2[:, 0:64], b21)
    m_ref[256:320, 256:384] = m2


def lower_product(m, high, low):
    out = []
    for rows, depth in (((0, 256), 256), ((256, 320), 320)):
        m_high, m_low = (part[rows[0] : rows[1], 0:depth] for part in m)
        x_high, x_low = high[0:depth], low[0:depth]
        out.append(mxu(m_high, x_high) + (mxu(m_high, x_low) + mxu(m_low, x_high)))
    return out


def factor_kernel(core_ref, half_ref, far_ref, m_ref, scratch):
    core = core_ref[0]
    own = half_ref[:, half_ref.shape[1] - 16 :, :].reshape(256, LANES)
    far = far_ref[...].reshape(256, LANES)
    factor(jnp.where(core == 0, own, far), jnp.where(core == 0, far, own), m_ref, scratch)


def finish_kernel(
    scale, core_ref, m_ref, half_ref, other_ref, high_hbm, mid_hbm, basis_hbm, proj_hbm,
    high, mid, basis, proj, in_sems, basis_sems, proj_sems,
):
    core = core_ref[0]
    tall, width = proj.shape
    rows = basis.shape[1]
    high_copy = pltpu.make_async_copy(high_hbm, high, in_sems.at[0])
    mid_copy = pltpu.make_async_copy(mid_hbm, mid, in_sems.at[1])
    high_copy.start()
    mid_copy.start()
    inverse = bf16_parts(m_ref[:, 0:tall])
    scaled = bf16_parts(m_ref[:, 0:tall] * scale)
    steps = width // 512

    def proj_copy(which, c):
        at = pl.multiple_of(which * (width // 2) + c * 256, 256)
        part = (slice(None), pl.ds(at, 256))
        number = which * steps + c
        return at, pltpu.make_async_copy(proj.at[part], proj_hbm.at[part], proj_sems.at[number])

    for ref, which in ((half_ref, core), (other_ref, 1 - core)):

        @pl.loop(0, steps)
        def _(c, ref=ref, which=which):
            tiles = ref[pl.ds(4 * c, 4), 0 : tall // 2, :].reshape(2, tall, LANES)
            cross = jnp.concatenate([tiles[0], tiles[1]], axis=1)
            at, move = proj_copy(which, c)
            upper, lower = lower_product(scaled, *bf16_parts(cross))
            proj[0:256, pl.ds(at, 256)] = upper
            proj[256:320, pl.ds(at, 256)] = lower
            move.start()

    high_copy.wait()
    mid_copy.wait()
    block = rows // BLOCKS

    def basis_copy(i):
        part = (slice(None), pl.ds(pl.multiple_of(i * block, block), block))
        return pltpu.make_async_copy(basis.at[part], basis_hbm.at[part], basis_sems.at[i])

    @pl.loop(0, BLOCKS)
    def _(i):
        part = pl.ds(pl.multiple_of(i * block, block), block)
        upper, lower = lower_product(inverse, high[:, part], mid[:, part])
        basis[0:256, part] = upper
        basis[256:320, part] = lower
        basis_copy(i).start()

    for which in range(2):

        @pl.loop(0, steps)
        def _(c, which=which):
            proj_copy(which, c)[1].wait()

    @pl.loop(0, BLOCKS)
    def _(i):
        basis_copy(i).wait()


def shards(latents, test_matrix):
    rows, width = latents.shape
    tall = test_matrix.shape[1]
    row_total = rows * lax.axis_size("blk") * lax.axis_size("inner")
    core = (lax.axis_index("blk") % 2).astype(jnp.int32).reshape(1)
    swap = [(i, i ^ 1) for i in range(2 * CHIPS)]
    groups = [[2 * i + side for i in range(CHIPS)] for side in range(2)]

    def over_chips(value):
        return lax.all_to_all(value, "blk", 0, 0, axis_index_groups=groups)

    high, mid, keep, give = front(core, latents, test_matrix.T, row_total)
    chunks = over_chips(keep + lax.ppermute(give, "blk", swap))
    chunk = lax.all_to_all(sum_copies(chunks, DEPTH), "inner", 0, 0)
    half = over_chips(sum_copies(chunk, CHIPS))
    gram_far = lax.ppermute(half[:, tall // 2 :], "blk", swap)
    half, gram_far = lax.optimization_barrier((half, gram_far))
    other = lax.ppermute(half, "blk", swap)
    inverse = call(
        factor_kernel,
        "factor",
        shape(tall, 384),
        [SMEM, VMEM, VMEM],
        VMEM,
        [pltpu.VMEM((9 * LANES, LANES), jnp.float32)],
        flops=12 * 10**9,
    )(core, half, gram_far)
    bf16 = jnp.bfloat16
    basis_t, projection = call(
        functools.partial(finish_kernel, float(width) ** 0.5 / row_total),
        "finish",
        [shape(tall, rows), shape(tall, width)],
        [SMEM, VMEM, VMEM, VMEM, HBM, HBM],
        [HBM, HBM],
        [
            pltpu.VMEM((tall, rows), bf16),
            pltpu.VMEM((tall, rows), bf16),
            pltpu.VMEM((tall, rows), jnp.float32),
            pltpu.VMEM((tall, width), jnp.float32),
            pltpu.SemaphoreType.DMA((2,)),
            pltpu.SemaphoreType.DMA((BLOCKS,)),
            pltpu.SemaphoreType.DMA((width // 256,)),
        ],
        flops=3 * 10**9,
        moved=10**7,
    )(core, inverse, half, other, high, mid)
    return (basis_t.T, projection)


def solution(mesh):
    placed = (P(("blk", "inner"), None), P())
    return jax.shard_map(
        shards,
        mesh=mesh,
        in_specs=placed,
        out_specs=(P(("blk", "inner"), None), P()),
        check_vma=False,
    )
```

time: 418 us -> 115 us (0.28)
  the two profiles are of different devices: /device:TPU:2 before, /device:TPU:1 now
where the time goes in v2:
time: 115 us; the launch traced here: 114 us
  blocking collectives  72.8 us (63%)
  Pallas kernels  26.5 us (23%)
  starting transfers between devices  8.91 us (8%)
  waiting for transfers between devices  3.84 us (3%)
  local copies, waits for them, and re-layouts  1.32 us (1%)
    all_to_all x2, blocking collectives, over_chips(): return lax.all_to_all(value, 'blk', 0, 0, axis_index_groups=groups)  46.2 us
    all_to_all x1, blocking collectives, shards(): chunk = lax.all_to_all(sum_copies(chunks, DEPTH), 'inner', 0, 0)  26.6 us
    pallas_call x1, Pallas kernels, front(): call(functools.partial(front_kernel, row_total), 'front', [shape(tall, ro...  10.4 us
    pallas_call x1, Pallas kernels, shards(): call(factor_kernel, 'factor', shape(tall, 384), [SMEM, VMEM, VMEM], VMEM,...  9.41 us
    pallas_call x1, Pallas kernels, shards(): call(functools.partial(finish_kernel, float(width) ** 0.5 / row_total), '...  6.55 us
    ppermute x1, starting transfers between devices, shards(): gram_far = lax.ppermute(half[:, tall // 2:], 'blk', swap)  5.21 us
    ppermute x1, starting transfers between devices, shards(): chunks = over_chips(keep + lax.ppermute(give, 'blk', swap))  3.33 us
    ppermute x1, waiting for transfers between devices, shards(): chunks = over_chips(keep + lax.ppermute(give, 'blk', swap))  2.85 us
  transfers between devices with their start and end apart: 3, of which 2 were waited for; matrix products, arithmetic and copies ran while one was open for 0% of the time, Pallas kernels for 8%

profile of v2, /device:TPU:1, one launch (start us, length us, event | category | flops | bytes accessed | tf_op | source)
XLA Modules:
  0.0 114.5 jit_solution(6237846270429140032)
XLA Ops:
  0.6 0.0 copy-start
  0.7 1.3 %copy-done = bf16[2048,320]{0,1:T(8,128)(2,1)S(1)} copy-done((bf16[2048,320]{0,1:T(8,128)(2,1)S(1)}, bf16[2048,320]{0,1:T(8,128)(2,1)}, u32[]{:S(2)}) %copy-start) | copy-done | bytes 1310744
  2.0 10.4 %front.1 = (bf16[320,1536]{1,0:T(8,128)(2,1)S(1)}, bf16[320,1536]{1,0:T(8,128)(2,1)S(1)}, f32[16,176,128]{2,1,0:T(8,128)S(1)}, f32[16,176,128]{2,1,0:T(8,128)S(1)}) custom-call(s32[1]{0:T(128)} %bitcast.core_ref, bf16[1536,2048]{1,0:T(8,128)(2,1)} %lat_hbm.1, bf16[320,2048]{1,0:T(8,128)(2,1)S(1)} %bitcast.3), custom_call_target="tpu_custom_call" | custom-call | flops 6000000000 | bytes 10000000 | tf_op jit(solution)/shard_map/front/pallas_call | solution.py:176
  12.3 3.3 %collective-permute-start = (f32[16,176,128]{2,1,0:T(8,128)S(1)}, f32[16,176,128]{2,1,0:T(8,128)S(1)}, u32[]{:S(2)}, u32[]{:S(2)}) collective-permute-start(f32[16,176,128]{2,1,0:T(8,128)S(1)} %get-tuple-element.11), channel_id=1, source_target_pairs={{0,8},{8,0},{16,24},{24,16},{32,40},{40,32},{48,56},{56,48},{64,72... | collective-permute-start | bytes 4325384 | tf_op jit(solution)/shard_map/ppermute | solution.py:328
  15.7 2.8 %collective-permute-done = f32[16,176,128]{2,1,0:T(8,128)S(1)} collective-permute-done((f32[16,176,128]{2,1,0:T(8,128)S(1)}, f32[16,176,128]{2,1,0:T(8,128)S(1)}, u32[]{:S(2)}, u32[]{:S(2)}) %collective-permute-start) | collective-permute-done | bytes 1441824 | tf_op jit(solution)/shard_map/ppermute | solution.py:328
  18.5 0.2 add.8
  18.8 24.5 %all_to_all.15.x_ref = f32[16,176,128]{2,1,0:T(8,128)S(1)} all-to-all(f32[16,176,128]{2,1,0:T(8,128)S(1)} %add.8), channel_id=1, replica_groups={{0,16,32,48,64,80,96,112,128,144,160,176,192,208,224,240},{8,24,40,56,7..., dimensions={0} | all-to-all | bytes 2883584 | tf_op jit(solution)/shard_map/all_to_all | solution.py:325
  43.3 0.1 sum_copies.2
  43.4 26.6 %all_to_all.16.x_ref = f32[8,176,128]{2,1,0:T(8,128)S(1)} all-to-all(f32[8,176,128]{2,1,0:T(8,128)S(1)} %sum_copies.2), channel_id=1, replica_groups=mesh['blk'=32,'inner'=8] {'inner'}, dimensions={0} | all-to-all | bytes 1441792 | tf_op jit(solution)/shard_map/all_to_all | solution.py:329
  70.0 0.1 sum_copies.3
  70.1 21.7 %all_to_all.17.half_ref = f32[16,176,128]{2,1,0:T(8,128)S(1)} all-to-all(f32[16,176,128]{2,1,0:T(8,128)S(1)} %sum_copies.3), channel_id=1, replica_groups={{0,16,32,48,64,80,96,112,128,144,160,176,192,208,224,240},{8,24,40,56,7..., dimensions={0} | all-to-all | bytes 2883584 | tf_op jit(solution)/shard_map/all_to_all | solution.py:325
  91.8 5.2 %collective-permute-start.1 = (f32[16,16,128]{2,1,0:T(8,128)S(1)}, f32[16,16,128]{2,1,0:T(8,128)S(1)}, u32[]{:S(2)}, u32[]{:S(2)}) collective-permute-start(f32[16,16,128]{2,1,0:T(8,128)S(1)} %slice.4), channel_id=1, source_target_pairs={{0,8},{8,0},{16,24},{24,16},{32,40},{40,32},{48,56},{56,48},{64,72... | collective-permute-start | bytes 393224 | tf_op jit(solution)/shard_map/ppermute | solution.py:331
  97.0 1.0 collective-permute-done.1.far_ref
  98.0 0.4 collective-permute-start.2
  98.4 9.4 %factor.1.m_ref = f32[320,384]{1,0:T(8,128)S(1)} custom-call(s32[1]{0:T(128)} %bitcast.core_ref, f32[16,176,128]{2,1,0:T(8,128)S(1)} %all_to_all.17.half_ref, f32[16,16,128]{2,1,0:T(8,128)S(1)} %collective-permute-done.1.far_ref), custom_call_target="tpu_custom_call" | custom-call | flops 12000000000 | bytes 1000000 | tf_op jit(solution)/shard_map/factor/pallas_call | solution.py:334
  107.8 0.0 collective-permute-done.2.other_ref
  107.8 6.5 %finish.1 = (f32[320,1536]{1,0:T(8,128)}, f32[320,2048]{1,0:T(8,128)}) custom-call(s32[1]{0:T(128)} %bitcast.core_ref, f32[320,384]{1,0:T(8,128)S(1)} %factor.1.m_ref, f32[16,176,128]{2,1,0:T(8,128)S(1)} %all_to_all.17.half_ref, f32[16,176,128]{2,1,0:T(8,128)S(1)} %collective-permute-done.2.other_ref, bf16[320,1536]{1,0:T(8,128)(2,1)S(1)} %get-tuple-element.14.high_hbm, ...), custom_call_target="tpu_custom_call" | custom-call | flops 3000000000 | bytes 10000000 | tf_op jit(solution)/shard_map/finish/pallas_call | solution.py:344
  (1 shorter events, 0.0 us)
Async XLA Ops:
  0.6 1.3 %copy-start = (bf16[2048,320]{0,1:T(8,128)(2,1)S(1)}, bf16[2048,320]{0,1:T(8,128)(2,1)}, u32[]{:S(2)}) copy-start(bf16[2048,320]{0,1:T(8,128)(2,1)} %param.3) | copy-start | bytes 3932164
  12.3 6.2 %collective-permute-start = (f32[16,176,128]{2,1,0:T(8,128)S(1)}, f32[16,176,128]{2,1,0:T(8,128)S(1)}, u32[]{:S(2)}, u32[]{:S(2)}) collective-permute-start(f32[16,176,128]{2,1,0:T(8,128)S(1)} %get-tuple-element.11), channel_id=1, source_target_pairs={{0,8},{8,0},{16,24},{24,16},{32,40},{40,32},{48,56},{56,48},{64,72... | collective-permute-start | bytes 4325384 | tf_op jit(solution)/shard_map/ppermute | solution.py:328
  91.8 6.2 %collective-permute-start.1 = (f32[16,16,128]{2,1,0:T(8,128)S(1)}, f32[16,16,128]{2,1,0:T(8,128)S(1)}, u32[]{:S(2)}, u32[]{:S(2)}) collective-permute-start(f32[16,16,128]{2,1,0:T(8,128)S(1)} %slice.4), channel_id=1, source_target_pairs={{0,8},{8,0},{16,24},{24,16},{32,40},{40,32},{48,56},{56,48},{64,72... | collective-permute-start | bytes 393224 | tf_op jit(solution)/shard_map/ppermute | solution.py:331
  98.0 9.8 %collective-permute-start.2 = (f32[16,176,128]{2,1,0:T(8,128)S(1)}, f32[16,176,128]{2,1,0:T(8,128)S(1)}, u32[]{:S(2)}, u32[]{:S(2)}) collective-permute-start(f32[16,176,128]{2,1,0:T(8,128)S(1)} %all_to_all.17.half_ref), channel_id=1, source_target_pairs={{0,8},{8,0},{16,24},{24,16},{32,40},{40,32},{48,56},{56,48},{64,72... | collective-permute-start | bytes 4325384 | tf_op jit(solution)/shard_map/ppermute | solution.py:333

commit v3 on v2

--- a/solution.py
+++ b/solution.py
@@ -95,7 +95,8 @@
 HBM = pl.BlockSpec(memory_space=pltpu.HBM)
 CHIPS = 16
 DEPTH = 8
-BLOCKS = 6
+BLOCKS = 3
+LOADS = 3
 
 
 def shape(*dims, dtype=jnp.float32):
@@ -116,48 +117,48 @@
 
 
 def front_kernel(
-    row_total, core_ref, lat_hbm, om_hbm, high_ref, mid_ref, keep_ref, give_ref, lat, om_ref, low, sems
+    row_total, core_ref, lat_hbm, om_hbm, high_ref, mid_ref, keep_ref, give_ref, lat, om, parts, sems
 ):
     rows, width = lat.shape
-    tall = om_ref.shape[0]
-    block = rows // BLOCKS
+    tall = om.shape[0]
+    block = rows // LOADS
     core = core_ref[0]
 
     def load(i):
-        part = pl.ds(pl.multiple_of(i * block, block), block)
+        part = pl.ds(i * block, block)
         return pltpu.make_async_copy(lat_hbm.at[part], lat.at[part], sems.at[i])
 
-    test = pltpu.make_async_copy(om_hbm, om_ref, sems.at[BLOCKS])
+    test = pltpu.make_async_copy(om_hbm, om, sems.at[LOADS])
     test.start()
-    for i in range(BLOCKS):
+    for i in range(LOADS):
         load(i).start()
     test.wait()
-
-    @pl.loop(0, BLOCKS)
-    def _(i):
+    for i in range(LOADS):
         load(i).wait()
-        part = pl.ds(pl.multiple_of(i * block, block), block)
-        s = mxu(om_ref[...], lat[part, :], ROWS_OF)
+        part = pl.ds(i * block, block)
+        s = mxu(om[...], lat[part, :], ROWS_OF)
         high, mid = bf16_parts(s)
+        low = (s - high.astype(jnp.float32) - mid.astype(jnp.float32)).astype(jnp.bfloat16)
         high_ref[:, part] = high
         mid_ref[:, part] = mid
-        low[:, part] = (s - high.astype(jnp.float32) - mid.astype(jnp.float32)).astype(jnp.bfloat16)
+        parts[0:tall, part] = high
+        parts[tall : 2 * tall, part] = mid
+        parts[2 * tall :, part] = low
 
     for ref, which in ((give_ref, 1 - core), (keep_ref, core)):
-
-        @pl.loop(0, width // 512)
-        def _(c, ref=ref, which=which):
-            at = pl.multiple_of(which * (width // 2) + c * 256, 256)
-            out = mxu(high_ref[...], lat[:, pl.ds(at, 256)])
-            for k in range(4):
-                piece = out[(k % 2) * (tall // 2) : (k % 2 + 1) * (tall // 2)]
-                piece = piece[:, (k // 2) * LANES : (k // 2 + 1) * LANES]
-                ref[4 * c + k, 0 : tall // 2, :] = piece
-
-    high = high_ref[...]
-    mid = mid_ref[...]
-    cross_mid = mxu(high, mid, ROWS_OF) + mxu(high, low[...], ROWS_OF)
-    gram = mxu(high, high, ROWS_OF) + (cross_mid + cross_mid.T + mxu(mid, mid, ROWS_OF))
+        at = pl.multiple_of(which * (width // 2), width // 2)
+        out = mxu(parts[0:tall, :], lat[:, pl.ds(at, width // 2)])
+        for j in range(CHIPS):
+            rows_from = (j % 2) * (tall // 2)
+            lanes_from = (j // 2) * LANES
+            ref[j, 0 : tall // 2, :] = out[
+                rows_from : rows_from + tall // 2, lanes_from : lanes_from + LANES
+            ]
+
+    by_high = mxu(parts[0:tall, :], parts[...], ROWS_OF)
+    mixed = by_high[:, tall : 2 * tall] + by_high[:, 2 * tall :]
+    mid = parts[tall : 2 * tall, :]
+    gram = by_high[:, 0:tall] + (mixed + mixed.T + mxu(mid, mid, ROWS_OF))
     gram = gram * (1.0 / row_total)
     corner = jnp.concatenate([gram[256:320, 256:320], gram[64:128, 64:128]], axis=1)
     zero = jnp.concatenate([gram[0:64, 0:128], corner, gram[0:128, 128:256]], axis=0)
@@ -187,8 +188,8 @@
         [
             pltpu.VMEM((rows, width), bf16),
             pltpu.VMEM((tall, width), bf16),
-            pltpu.VMEM((tall, rows), bf16),
-            pltpu.SemaphoreType.DMA((BLOCKS + 1,)),
+            pltpu.VMEM((3 * tall, rows), bf16),
+            pltpu.SemaphoreType.DMA((LOADS + 1,)),
         ],
         flops=6 * 10**9,
         moved=10**7,
@@ -265,52 +266,36 @@
     high_copy.start()
     mid_copy.start()
     inverse = bf16_parts(m_ref[:, 0:tall])
-    scaled = bf16_parts(m_ref[:, 0:tall] * scale)
-    steps = width // 512
-
-    def proj_copy(which, c):
-        at = pl.multiple_of(which * (width // 2) + c * 256, 256)
-        part = (slice(None), pl.ds(at, 256))
-        number = which * steps + c
-        return at, pltpu.make_async_copy(proj.at[part], proj_hbm.at[part], proj_sems.at[number])
-
-    for ref, which in ((half_ref, core), (other_ref, 1 - core)):
-
-        @pl.loop(0, steps)
-        def _(c, ref=ref, which=which):
-            tiles = ref[pl.ds(4 * c, 4), 0 : tall // 2, :].reshape(2, tall, LANES)
-            cross = jnp.concatenate([tiles[0], tiles[1]], axis=1)
-            at, move = proj_copy(which, c)
-            upper, lower = lower_product(scaled, *bf16_parts(cross))
-            proj[0:256, pl.ds(at, 256)] = upper
-            proj[256:320, pl.ds(at, 256)] = lower
-            move.start()
-
+    step = width // 4
+    copies = []
+    for c in range(4):
+        ref, which = (half_ref, core) if c < 2 else (other_ref, 1 - core)
+        tiles = ref[8 * (c % 2) : 8 * (c % 2) + 8, 0 : tall // 2, :].reshape(4, tall, LANES)
+        cross = jnp.concatenate([tiles[i] for i in range(4)], axis=1)
+        upper, lower = lower_product(inverse, *bf16_parts(cross))
+        proj[0:256, c * step : (c + 1) * step] = upper * scale
+        proj[256:320, c * step : (c + 1) * step] = lower * scale
+        there = pl.ds(pl.multiple_of(which * (2 * step) + (c % 2) * step, step), step)
+        copies.append(
+            pltpu.make_async_copy(
+                proj.at[:, pl.ds(c * step, step)], proj_hbm.at[:, there], proj_sems.at[c]
+            )
+        )
+        copies[-1].start()
     high_copy.wait()
     mid_copy.wait()
     block = rows // BLOCKS
-
-    def basis_copy(i):
-        part = (slice(None), pl.ds(pl.multiple_of(i * block, block), block))
-        return pltpu.make_async_copy(basis.at[part], basis_hbm.at[part], basis_sems.at[i])
-
-    @pl.loop(0, BLOCKS)
-    def _(i):
-        part = pl.ds(pl.multiple_of(i * block, block), block)
+    for i in range(BLOCKS):
+        part = pl.ds(i * block, block)
         upper, lower = lower_product(inverse, high[:, part], mid[:, part])
         basis[0:256, part] = upper
         basis[256:320, part] = lower
-        basis_copy(i).start()
-
-    for which in range(2):
-
-        @pl.loop(0, steps)
-        def _(c, which=which):
-            proj_copy(which, c)[1].wait()
-
-    @pl.loop(0, BLOCKS)
-    def _(i):
-        basis_copy(i).wait()
+        copies.append(
+            pltpu.make_async_copy(basis.at[:, part], basis_hbm.at[:, part], basis_sems.at[i])
+        )
+        copies[-1].start()
+    for copy in copies:
+        copy.wait()
 
 
 def shards(latents, test_matrix):
@@ -354,7 +339,7 @@
             pltpu.VMEM((tall, width), jnp.float32),
             pltpu.SemaphoreType.DMA((2,)),
             pltpu.SemaphoreType.DMA((BLOCKS,)),
-            pltpu.SemaphoreType.DMA((width // 256,)),
+            pltpu.SemaphoreType.DMA((4,)),
         ],
         flops=3 * 10**9,
         moved=10**7,

time: 115 us -> 111 us (0.965)
  Pallas kernels: 26.5 us -> 22.7 us
    pallas_call x1, Pallas kernels: 10.4 us -> 8.35 us  [front(): call(functools.partial(front_kernel, row_total), 'front', [shape(tall, ro...]
    pallas_call x1, Pallas kernels: 6.55 us -> 4.73 us  [shards(): call(functools.partial(finish_kernel, float(width) ** 0.5 / row_total), '...]
  transfers between devices with their start and end apart: 3 -> 3, of which waited for: 2 -> 2; matrix products, arithmetic and copies ran while one was open for 0% -> 0% of each run, Pallas kernels for 8% -> 9%
where the time goes in v3:
time: 111 us
  blocking collectives  72.8 us (66%)
  Pallas kernels  22.7 us (20%)
  starting transfers between devices  8.91 us (8%)
  waiting for transfers between devices  3.84 us (3%)
  local copies, waits for them, and re-layouts  1.32 us (1%)
    all_to_all x2, blocking collectives, over_chips(): return lax.all_to_all(value, 'blk', 0, 0, axis_index_groups=groups)  46.2 us
    all_to_all x1, blocking collectives, shards(): chunk = lax.all_to_all(sum_copies(chunks, DEPTH), 'inner', 0, 0)  26.6 us
    pallas_call x1, Pallas kernels, shards(): call(factor_kernel, 'factor', shape(tall, 384), [SMEM, VMEM, VMEM], VMEM,...  9.41 us
    pallas_call x1, Pallas kernels, front(): call(functools.partial(front_kernel, row_total), 'front', [shape(tall, ro...  8.35 us
    ppermute x1, starting transfers between devices, shards(): gram_far = lax.ppermute(half[:, tall // 2:], 'blk', swap)  5.21 us
    pallas_call x1, Pallas kernels, shards(): call(functools.partial(finish_kernel, float(width) ** 0.5 / row_total), '...  4.73 us
    ppermute x1, starting transfers between devices, shards(): chunks = over_chips(keep + lax.ppermute(give, 'blk', swap))  3.33 us
    ppermute x1, waiting for transfers between devices, shards(): chunks = over_chips(keep + lax.ppermute(give, 'blk', swap))  2.85 us
  transfers between devices with their start and end apart: 3, of which 2 were waited for; matrix products, arithmetic and copies ran while one was open for 0% of the time, Pallas kernels for 9%

profile of v3, /device:TPU:1, one launch (start us, length us, event | category | flops | bytes accessed | tf_op | source)
XLA Modules:
  0.0 110.6 jit_solution(14265222276543324117)
XLA Ops:
  0.6 0.0 copy-start
  0.7 1.3 %copy-done = bf16[2048,320]{0,1:T(8,128)(2,1)S(1)} copy-done((bf16[2048,320]{0,1:T(8,128)(2,1)S(1)}, bf16[2048,320]{0,1:T(8,128)(2,1)}, u32[]{:S(2)}) %copy-start) | copy-done | bytes 1310744
  2.0 8.3 %front.1 = (bf16[320,1536]{1,0:T(8,128)(2,1)S(1)}, bf16[320,1536]{1,0:T(8,128)(2,1)S(1)}, f32[16,176,128]{2,1,0:T(8,128)S(1)}, f32[16,176,128]{2,1,0:T(8,128)S(1)}) custom-call(s32[1]{0:T(128)} %bitcast.core_ref, bf16[1536,2048]{1,0:T(8,128)(2,1)} %lat_hbm.1, bf16[320,2048]{1,0:T(8,128)(2,1)S(1)} %bitcast.3), custom_call_target="tpu_custom_call" | custom-call | flops 6000000000 | bytes 10000000 | tf_op jit(solution)/shard_map/front/pallas_call | solution.py:177
  10.3 3.3 %collective-permute-start = (f32[16,176,128]{2,1,0:T(8,128)S(1)}, f32[16,176,128]{2,1,0:T(8,128)S(1)}, u32[]{:S(2)}, u32[]{:S(2)}) collective-permute-start(f32[16,176,128]{2,1,0:T(8,128)S(1)} %get-tuple-element.11), channel_id=1, source_target_pairs={{0,8},{8,0},{16,24},{24,16},{32,40},{40,32},{48,56},{56,48},{64,72... | collective-permute-start | bytes 4325384 | tf_op jit(solution)/shard_map/ppermute | solution.py:313
  13.7 2.8 %collective-permute-done = f32[16,176,128]{2,1,0:T(8,128)S(1)} collective-permute-done((f32[16,176,128]{2,1,0:T(8,128)S(1)}, f32[16,176,128]{2,1,0:T(8,128)S(1)}, u32[]{:S(2)}, u32[]{:S(2)}) %collective-permute-start) | collective-permute-done | bytes 1441824 | tf_op jit(solution)/shard_map/ppermute | solution.py:313
  16.5 0.2 add.8
  16.7 24.5 %all_to_all.15.x_ref = f32[16,176,128]{2,1,0:T(8,128)S(1)} all-to-all(f32[16,176,128]{2,1,0:T(8,128)S(1)} %add.8), channel_id=1, replica_groups={{0,16,32,48,64,80,96,112,128,144,160,176,192,208,224,240},{8,24,40,56,7..., dimensions={0} | all-to-all | bytes 2883584 | tf_op jit(solution)/shard_map/all_to_all | solution.py:310
  41.2 0.1 sum_copies.2
  41.3 26.6 %all_to_all.16.x_ref = f32[8,176,128]{2,1,0:T(8,128)S(1)} all-to-all(f32[8,176,128]{2,1,0:T(8,128)S(1)} %sum_copies.2), channel_id=1, replica_groups=mesh['blk'=32,'inner'=8] {'inner'}, dimensions={0} | all-to-all | bytes 1441792 | tf_op jit(solution)/shard_map/all_to_all | solution.py:314
  67.9 0.1 sum_copies.3
  68.1 21.7 %all_to_all.17.half_ref = f32[16,176,128]{2,1,0:T(8,128)S(1)} all-to-all(f32[16,176,128]{2,1,0:T(8,128)S(1)} %sum_copies.3), channel_id=1, replica_groups={{0,16,32,48,64,80,96,112,128,144,160,176,192,208,224,240},{8,24,40,56,7..., dimensions={0} | all-to-all | bytes 2883584 | tf_op jit(solution)/shard_map/all_to_all | solution.py:310
  89.8 5.2 %collective-permute-start.1 = (f32[16,16,128]{2,1,0:T(8,128)S(1)}, f32[16,16,128]{2,1,0:T(8,128)S(1)}, u32[]{:S(2)}, u32[]{:S(2)}) collective-permute-start(f32[16,16,128]{2,1,0:T(8,128)S(1)} %slice.4), channel_id=1, source_target_pairs={{0,8},{8,0},{16,24},{24,16},{32,40},{40,32},{48,56},{56,48},{64,72... | collective-permute-start | bytes 393224 | tf_op jit(solution)/shard_map/ppermute | solution.py:316
  95.0 1.0 collective-permute-done.1.far_ref
  96.0 0.4 collective-permute-start.2
  96.3 9.4 %factor.1.m_ref = f32[320,384]{1,0:T(8,128)S(1)} custom-call(s32[1]{0:T(128)} %bitcast.core_ref, f32[16,176,128]{2,1,0:T(8,128)S(1)} %all_to_all.17.half_ref, f32[16,16,128]{2,1,0:T(8,128)S(1)} %collective-permute-done.1.far_ref), custom_call_target="tpu_custom_call" | custom-call | flops 12000000000 | bytes 1000000 | tf_op jit(solution)/shard_map/factor/pallas_call | solution.py:319
  105.7 0.0 collective-permute-done.2.other_ref
  105.8 4.7 %finish.1 = (f32[320,1536]{1,0:T(8,128)}, f32[320,2048]{1,0:T(8,128)}) custom-call(s32[1]{0:T(128)} %bitcast.core_ref, f32[320,384]{1,0:T(8,128)S(1)} %factor.1.m_ref, f32[16,176,128]{2,1,0:T(8,128)S(1)} %all_to_all.17.half_ref, f32[16,176,128]{2,1,0:T(8,128)S(1)} %collective-permute-done.2.other_ref, bf16[320,1536]{1,0:T(8,128)(2,1)S(1)} %get-tuple-element.14.high_hbm, ...), custom_call_target="tpu_custom_call" | custom-call | flops 3000000000 | bytes 10000000 | tf_op jit(solution)/shard_map/finish/pallas_call | solution.py:329
  (1 shorter events, 0.0 us)
Async XLA Ops:
  0.6 1.3 %copy-start = (bf16[2048,320]{0,1:T(8,128)(2,1)S(1)}, bf16[2048,320]{0,1:T(8,128)(2,1)}, u32[]{:S(2)}) copy-start(bf16[2048,320]{0,1:T(8,128)(2,1)} %param.3) | copy-start | bytes 3932164
  10.3 6.2 %collective-permute-start = (f32[16,176,128]{2,1,0:T(8,128)S(1)}, f32[16,176,128]{2,1,0:T(8,128)S(1)}, u32[]{:S(2)}, u32[]{:S(2)}) collective-permute-start(f32[16,176,128]{2,1,0:T(8,128)S(1)} %get-tuple-element.11), channel_id=1, source_target_pairs={{0,8},{8,0},{16,24},{24,16},{32,40},{40,32},{48,56},{56,48},{64,72... | collective-permute-start | bytes 4325384 | tf_op jit(solution)/shard_map/ppermute | solution.py:313
  89.8 6.2 %collective-permute-start.1 = (f32[16,16,128]{2,1,0:T(8,128)S(1)}, f32[16,16,128]{2,1,0:T(8,128)S(1)}, u32[]{:S(2)}, u32[]{:S(2)}) collective-permute-start(f32[16,16,128]{2,1,0:T(8,128)S(1)} %slice.4), channel_id=1, source_target_pairs={{0,8},{8,0},{16,24},{24,16},{32,40},{40,32},{48,56},{56,48},{64,72... | collective-permute-start | bytes 393224 | tf_op jit(solution)/shard_map/ppermute | solution.py:316
  96.0 9.8 %collective-permute-start.2 = (f32[16,176,128]{2,1,0:T(8,128)S(1)}, f32[16,176,128]{2,1,0:T(8,128)S(1)}, u32[]{:S(2)}, u32[]{:S(2)}) collective-permute-start(f32[16,176,128]{2,1,0:T(8,128)S(1)} %all_to_all.17.half_ref), channel_id=1, source_target_pairs={{0,8},{8,0},{16,24},{24,16},{32,40},{40,32},{48,56},{56,48},{64,72... | collective-permute-start | bytes 4325384 | tf_op jit(solution)/shard_map/ppermute | solution.py:318

commit v4 on v3

--- a/solution.py
+++ b/solution.py
@@ -95,7 +95,6 @@
 HBM = pl.BlockSpec(memory_space=pltpu.HBM)
 CHIPS = 16
 DEPTH = 8
-BLOCKS = 3
 LOADS = 3
 
 
@@ -116,8 +115,17 @@
     )
 
 
+def put_tiles(ref, first, out):
+    edge = out.shape[0] // 2
+    for j in range(out.shape[1] // LANES * 2):
+        rows_from, lanes_from = (j % 2) * edge, (j // 2) * LANES
+        ref[first + j, 0:edge, :] = out[
+            rows_from : rows_from + edge, lanes_from : lanes_from + LANES
+        ]
+
+
 def front_kernel(
-    row_total, core_ref, lat_hbm, om_hbm, high_ref, mid_ref, keep_ref, give_ref, lat, om, parts, sems
+    row_total, core_ref, lat_hbm, om_hbm, high_ref, mid_ref, own_ref, give_ref, lat, om, parts, sems
 ):
     rows, width = lat.shape
     tall = om.shape[0]
@@ -145,15 +153,8 @@
         parts[tall : 2 * tall, part] = mid
         parts[2 * tall :, part] = low
 
-    for ref, which in ((give_ref, 1 - core), (keep_ref, core)):
-        at = pl.multiple_of(which * (width // 2), width // 2)
-        out = mxu(parts[0:tall, :], lat[:, pl.ds(at, width // 2)])
-        for j in range(CHIPS):
-            rows_from = (j % 2) * (tall // 2)
-            lanes_from = (j // 2) * LANES
-            ref[j, 0 : tall // 2, :] = out[
-                rows_from : rows_from + tall // 2, lanes_from : lanes_from + LANES
-            ]
+    at = pl.multiple_of((1 - core) * (width // 2), width // 2)
+    put_tiles(give_ref, 0, mxu(parts[0:tall, :], lat[:, pl.ds(at, width // 2)]))
 
     by_high = mxu(parts[0:tall, :], parts[...], ROWS_OF)
     mixed = by_high[:, tall : 2 * tall] + by_high[:, 2 * tall :]
@@ -166,7 +167,7 @@
     one = jnp.concatenate([last, gram[128:256, 128:256]], axis=0)
     own = jnp.where(core == 0, zero, one).reshape(CHIPS, 16, LANES)
     far = jnp.where(core == 0, one, zero).reshape(CHIPS, 16, LANES)
-    keep_ref[:, tall // 2 :, :] = own
+    own_ref[...] = own
     give_ref[:, tall // 2 :, :] = far
 
 
@@ -180,7 +181,7 @@
         [
             shape(tall, rows, dtype=bf16),
             shape(tall, rows, dtype=bf16),
-            shape(CHIPS, tall // 2 + 16, LANES),
+            shape(CHIPS, 16, LANES),
             shape(CHIPS, tall // 2 + 16, LANES),
         ],
         [SMEM, HBM, HBM],
@@ -197,6 +198,37 @@
     )(core, latents, test_t)
 
 
+def keep_kernel(core_ref, lat_hbm, high_ref, own_ref, keep_ref, lat, sems):
+    width = lat.shape[2]
+    loads = []
+    for i in range(2):
+        at = pl.multiple_of(core_ref[0] * (2 * width) + i * width, width)
+        loads.append(
+            pltpu.make_async_copy(lat_hbm.at[:, pl.ds(at, width)], lat.at[i], sems.at[i])
+        )
+        loads[i].start()
+    keep_ref[:, high_ref.shape[0] // 2 :, :] = own_ref[...]
+    for i in range(2):
+        loads[i].wait()
+        put_tiles(keep_ref, i * CHIPS // 2, mxu(high_ref[...], lat[i]))
+
+
+def keep_half(core, latents, high, own):
+    rows, width = latents.shape
+    tall = high.shape[0]
+    return call(
+        keep_kernel,
+        "keep",
+        shape(CHIPS, tall // 2 + 16, LANES),
+        [SMEM, HBM, VMEM, VMEM],
+        VMEM,
+        [pltpu.VMEM((2, rows, width // 4), jnp.bfloat16), pltpu.SemaphoreType.DMA((2,))],
+        flops=10**9,
+        moved=5 * 10**6,
+        mib=46,
+    )(core, latents, high, own)
+
+
 def sum_copies_kernel(x_ref, out_ref):
     total = x_ref[0]
     for i in range(1, x_ref.shape[0]):
@@ -209,7 +241,63 @@
     return call(sum_copies_kernel, "sum_copies", shape(count, *x.shape[1:]), [VMEM], VMEM)(x)
 
 
-def factor(zero, one, m_ref, scratch):
+def back_kernel(
+    scale, core_ref, half_ref, other_ref, high_hbm, mid_hbm, basis_hbm, proj_hbm,
+    high, low, basis, proj, scratch, in_sems, basis_sems, proj_sems,
+):
+    core = core_ref[0]
+    tall, width = proj.shape
+    rows = basis.shape[1]
+    edge = tall // 2
+    loads = [
+        pltpu.make_async_copy(high_hbm, high.at[:, pl.ds(0, rows)], in_sems.at[0]),
+        pltpu.make_async_copy(mid_hbm, low.at[:, pl.ds(0, rows)], in_sems.at[1]),
+    ]
+    for load in loads:
+        load.start()
+    own = half_ref[:, edge:, :].reshape(256, LANES)
+    far = other_ref[:, edge:, :].reshape(256, LANES)
+    zero = jnp.where(core == 0, own, far)
+    one = jnp.where(core == 0, far, own)
+    for side, ref in enumerate((half_ref, other_ref)):
+        for j in range(CHIPS):
+            here = pl.ds(rows + side * (width // 2) + (j // 2) * LANES, LANES)
+            part = pl.ds((j % 2) * edge, edge)
+            high[part, here], low[part, here] = bf16_parts(ref[j, 0:edge, :])
+
+    def product(first, m):
+        count, depth = m.shape
+        m_high, m_low = bf16_parts(m)
+        m_both = jnp.concatenate([m_high, m_low], axis=0)
+        for c in range((rows + width) // 512):
+            part = slice(512 * c, 512 * c + 512)
+            x_high, x_low = high[0:depth, part], low[0:depth, part]
+            by_high = mxu(m_both, x_high)
+            y = by_high[:count] + (mxu(m_high, x_low) + by_high[count:])
+            if 512 * c < rows:
+                basis[first : first + count, part] = y
+            else:
+                proj[first : first + count, 512 * c - rows : 512 * c + 512 - rows] = y * scale
+
+    copies = []
+
+    def send(i, first, count):
+        part = pl.ds(first, count)
+        copies.append(
+            pltpu.make_async_copy(basis.at[part], basis_hbm.at[part], basis_sems.at[i])
+        )
+        for side in range(2):
+            here = pl.ds(side * (width // 2), width // 2)
+            to = core if side == 0 else 1 - core
+            there = pl.ds(pl.multiple_of(to * (width // 2), width // 2), width // 2)
+            copies.append(
+                pltpu.make_async_copy(
+                    proj.at[part, here], proj_hbm.at[part, there], proj_sems.at[i, side]
+                )
+            )
+        for copy in copies[-3:]:
+            copy.start()
+
     left = jnp.concatenate([zero[0:64, 64:128].T, zero[64:128, 64:128]], axis=1)
     g00 = jnp.concatenate([zero[0:64], left], axis=0)
     blank = jnp.zeros((128, 64), jnp.float32)
@@ -217,83 +305,27 @@
     g12 = jnp.concatenate([one[0:128, 64:128], blank], axis=1)
     g22 = jnp.concatenate([zero[64:128, 0:64], blank[0:64]], axis=1)
     m0 = factor_inverse(g00, 128, scratch)
+    for load in loads:
+        load.wait()
     a01 = dot(m0, g01)
-    m_ref[0:128, 0:128] = m0
-    m_ref[0:128, 128:384] = jnp.zeros((128, 256), jnp.float32)
-    m1 = factor_inverse(one[128:256] - dot_t(a01[:, 0:128], a01[:, 0:128]), 128, scratch)
+    s11 = one[128:256] - dot_t(a01[:, 0:128], a01[:, 0:128])
+    product(0, m0)
+    m1 = factor_inverse(s11, 128, scratch)
     s12 = g12 - dot_t(a01[:, 0:128], a01[:, 128:256])
     s22 = g22 - dot_t(a01[:, 128:256], a01[:, 128:256])[0:64]
     b0 = -dot_t(a01, m0)
+    send(0, 0, 128)
     a12 = dot(m1, s12)
     s22 = s22 - dot_t(a12, a12)[0:64]
+    b10 = dot(m1, b0[0:128])
+    product(128, jnp.concatenate([b10, m1], axis=1))
     m2 = factor_inverse(s22, 64, scratch)
-    b10 = dot(m1, b0[0:128])
-    m_ref[128:256, 0:128] = b10
-    m_ref[128:256, 128:256] = m1
-    m_ref[128:256, 256:384] = jnp.zeros((128, 128), jnp.float32)
     b20 = b0[128:192] - dot_t(a12, b10)[0:64]
     b21 = -dot_t(a12, m1)[0:64]
-    m_ref[256:320, 0:128] = dot(m2[:, 0:64], b20)
-    m_ref[256:320, 128:256] = dot(m2[:, 0:64], b21)
-    m_ref[256:320, 256:384] = m2
-
-
-def lower_product(m, high, low):
-    out = []
-    for rows, depth in (((0, 256), 256), ((256, 320), 320)):
-        m_high, m_low = (part[rows[0] : rows[1], 0:depth] for part in m)
-        x_high, x_low = high[0:depth], low[0:depth]
-        out.append(mxu(m_high, x_high) + (mxu(m_high, x_low) + mxu(m_low, x_high)))
-    return out
-
-
-def factor_kernel(core_ref, half_ref, far_ref, m_ref, scratch):
-    core = core_ref[0]
-    own = half_ref[:, half_ref.shape[1] - 16 :, :].reshape(256, LANES)
-    far = far_ref[...].reshape(256, LANES)
-    factor(jnp.where(core == 0, own, far), jnp.where(core == 0, far, own), m_ref, scratch)
-
-
-def finish_kernel(
-    scale, core_ref, m_ref, half_ref, other_ref, high_hbm, mid_hbm, basis_hbm, proj_hbm,
-    high, mid, basis, proj, in_sems, basis_sems, proj_sems,
-):
-    core = core_ref[0]
-    tall, width = proj.shape
-    rows = basis.shape[1]
-    high_copy = pltpu.make_async_copy(high_hbm, high, in_sems.at[0])
-    mid_copy = pltpu.make_async_copy(mid_hbm, mid, in_sems.at[1])
-    high_copy.start()
-    mid_copy.start()
-    inverse = bf16_parts(m_ref[:, 0:tall])
-    step = width // 4
-    copies = []
-    for c in range(4):
-        ref, which = (half_ref, core) if c < 2 else (other_ref, 1 - core)
-        tiles = ref[8 * (c % 2) : 8 * (c % 2) + 8, 0 : tall // 2, :].reshape(4, tall, LANES)
-        cross = jnp.concatenate([tiles[i] for i in range(4)], axis=1)
-        upper, lower = lower_product(inverse, *bf16_parts(cross))
-        proj[0:256, c * step : (c + 1) * step] = upper * scale
-        proj[256:320, c * step : (c + 1) * step] = lower * scale
-        there = pl.ds(pl.multiple_of(which * (2 * step) + (c % 2) * step, step), step)
-        copies.append(
-            pltpu.make_async_copy(
-                proj.at[:, pl.ds(c * step, step)], proj_hbm.at[:, there], proj_sems.at[c]
-            )
-        )
-        copies[-1].start()
-    high_copy.wait()
-    mid_copy.wait()
-    block = rows // BLOCKS
-    for i in range(BLOCKS):
-        part = pl.ds(i * block, block)
-        upper, lower = lower_product(inverse, high[:, part], mid[:, part])
-        basis[0:256, part] = upper
-        basis[256:320, part] = lower
-        copies.append(
-            pltpu.make_async_copy(basis.at[:, part], basis_hbm.at[:, part], basis_sems.at[i])
-        )
-        copies[-1].start()
+    send(1, 128, 128)
+    m2 = m2[:, 0:64]
+    product(256, jnp.concatenate([dot(m2, b20), dot(m2, b21), m2], axis=1))
+    send(2, 256, 64)
     for copy in copies:
         copy.wait()
 
@@ -309,41 +341,32 @@
     def over_chips(value):
         return lax.all_to_all(value, "blk", 0, 0, axis_index_groups=groups)
 
-    high, mid, keep, give = front(core, latents, test_matrix.T, row_total)
-    chunks = over_chips(keep + lax.ppermute(give, "blk", swap))
+    high, mid, own, give = front(core, latents, test_matrix.T, row_total)
+    given = lax.ppermute(give, "blk", swap)
+    chunks = over_chips(keep_half(core, latents, high, own) + given)
     chunk = lax.all_to_all(sum_copies(chunks, DEPTH), "inner", 0, 0)
     half = over_chips(sum_copies(chunk, CHIPS))
-    gram_far = lax.ppermute(half[:, tall // 2 :], "blk", swap)
-    half, gram_far = lax.optimization_barrier((half, gram_far))
     other = lax.ppermute(half, "blk", swap)
-    inverse = call(
-        factor_kernel,
-        "factor",
-        shape(tall, 384),
-        [SMEM, VMEM, VMEM],
-        VMEM,
-        [pltpu.VMEM((9 * LANES, LANES), jnp.float32)],
-        flops=12 * 10**9,
-    )(core, half, gram_far)
     bf16 = jnp.bfloat16
     basis_t, projection = call(
-        functools.partial(finish_kernel, float(width) ** 0.5 / row_total),
-        "finish",
+        functools.partial(back_kernel, float(width) ** 0.5 / row_total),
+        "back",
         [shape(tall, rows), shape(tall, width)],
-        [SMEM, VMEM, VMEM, VMEM, HBM, HBM],
+        [SMEM, VMEM, VMEM, HBM, HBM],
         [HBM, HBM],
         [
-            pltpu.VMEM((tall, rows), bf16),
-            pltpu.VMEM((tall, rows), bf16),
+            pltpu.VMEM((tall, rows + width), bf16),
+            pltpu.VMEM((tall, rows + width), bf16),
             pltpu.VMEM((tall, rows), jnp.float32),
             pltpu.VMEM((tall, width), jnp.float32),
+            pltpu.VMEM((9 * LANES, LANES), jnp.float32),
             pltpu.SemaphoreType.DMA((2,)),
-            pltpu.SemaphoreType.DMA((BLOCKS,)),
-            pltpu.SemaphoreType.DMA((4,)),
+            pltpu.SemaphoreType.DMA((3,)),
+            pltpu.SemaphoreType.DMA((3, 2)),
         ],
         flops=3 * 10**9,
         moved=10**7,
-    )(core, inverse, half, other, high, mid)
+    )(core, half, other, high, mid)
     return (basis_t.T, projection)
 
 

time: 111 us -> 109 us (0.982)
    ppermute x2 -> x1, starting transfers between devices: 8.55 us -> 3.33 us  [shards(): given = lax.ppermute(give, 'blk', swap)]
    ppermute x1, starting transfers between devices: 0.36 us -> 5.13 us  [shards(): other = lax.ppermute(half, 'blk', swap)]
    ppermute x2 -> x1, waiting for transfers between devices: 3.84 us -> 0.07 us  [shards(): given = lax.ppermute(give, 'blk', swap)]
    ppermute x1, waiting for transfers between devices: 0.01 us -> 2.85 us  [shards(): other = lax.ppermute(half, 'blk', swap)]
  transfers between devices with their start and end apart: 3 -> 2, of which waited for: 2 -> 2; matrix products, arithmetic and copies ran while one was open for 0% -> 0% of each run, Pallas kernels for 9% -> 3%
where the time goes in v4:
time: 109 us; the launch traced here: 108 us
  blocking collectives  72.8 us (67%)
  Pallas kernels  21.9 us (20%)
  starting transfers between devices  8.46 us (8%)
  waiting for transfers between devices  2.92 us (3%)
  local copies, waits for them, and re-layouts  1.31 us (1%)
    all_to_all x2, blocking collectives, over_chips(): return lax.all_to_all(value, 'blk', 0, 0, axis_index_groups=groups)  46.2 us
    all_to_all x1, blocking collectives, shards(): chunk = lax.all_to_all(sum_copies(chunks, DEPTH), 'inner', 0, 0)  26.6 us
    pallas_call x1, Pallas kernels, shards(): call(functools.partial(back_kernel, float(width) ** 0.5 / row_total), 'ba...  11.7 us
    pallas_call x1, Pallas kernels, front(): call(functools.partial(front_kernel, row_total), 'front', [shape(tall, ro...  7.33 us
    ppermute x1, starting transfers between devices, shards(): other = lax.ppermute(half, 'blk', swap)  5.13 us
    ppermute x1, starting transfers between devices, shards(): given = lax.ppermute(give, 'blk', swap)  3.33 us
    ppermute x1, waiting for transfers between devices, shards(): other = lax.ppermute(half, 'blk', swap)  2.85 us
    pallas_call x1, Pallas kernels, keep_half(): call(keep_kernel, 'keep', shape(CHIPS, tall // 2 + 16, LANES), [SMEM, HBM...  2.77 us
  transfers between devices with their start and end apart: 2, of which 2 were waited for; matrix products, arithmetic and copies ran while one was open for 0% of the time, Pallas kernels for 3%

profile of v4, /device:TPU:1, one launch (start us, length us, event | category | flops | bytes accessed | tf_op | source)
XLA Modules:
  0.0 108.5 jit_solution(257255001211856544)
XLA Ops:
  0.6 0.0 copy-start
  0.7 1.3 %copy-done = bf16[2048,320]{0,1:T(8,128)(2,1)S(1)} copy-done((bf16[2048,320]{0,1:T(8,128)(2,1)S(1)}, bf16[2048,320]{0,1:T(8,128)(2,1)}, u32[]{:S(2)}) %copy-start) | copy-done | bytes 1310744
  2.0 7.3 %front.1 = (bf16[320,1536]{1,0:T(8,128)(2,1)S(1)}, bf16[320,1536]{1,0:T(8,128)(2,1)S(1)}, f32[16,16,128]{2,1,0:T(8,128)S(1)}, f32[16,176,128]{2,1,0:T(8,128)S(1)}) custom-call(s32[1]{0:T(128)} %bitcast.core_ref, bf16[1536,2048]{1,0:T(8,128)(2,1)} %lat_hbm.3, bf16[320,2048]{1,0:T(8,128)(2,1)S(1)} %bitcast.3), custom_call_target="tpu_custom_call" | custom-call | flops 6000000000 | bytes 10000000 | tf_op jit(solution)/shard_map/front/pallas_call | solution.py:178
  9.3 3.3 %collective-permute-start = (f32[16,176,128]{2,1,0:T(8,128)S(1)}, f32[16,176,128]{2,1,0:T(8,128)S(1)}, u32[]{:S(2)}, u32[]{:S(2)}) collective-permute-start(f32[16,176,128]{2,1,0:T(8,128)S(1)} %get-tuple-element.10), channel_id=1, source_target_pairs={{0,8},{8,0},{16,24},{24,16},{32,40},{40,32},{48,56},{56,48},{64,72... | collective-permute-start | bytes 4325384 | tf_op jit(solution)/shard_map/ppermute | solution.py:345
  12.6 2.8 %keep.1 = f32[16,176,128]{2,1,0:T(8,128)S(1)} custom-call(s32[1]{0:T(128)} %bitcast.core_ref, bf16[1536,2048]{1,0:T(8,128)(2,1)} %lat_hbm.3, bf16[320,1536]{1,0:T(8,128)(2,1)S(1)} %get-tuple-element.8.high_ref.high_hbm, f32[16,16,128]{2,1,0:T(8,128)S(1)} %get-tuple-element.9.own_ref), custom_call_target="tpu_custom_call" | custom-call | flops 1000000000 | bytes 5000000 | tf_op jit(solution)/shard_map/keep/pallas_call | solution.py:219
  15.4 0.1 collective-permute-done
  15.5 0.1 add.8
  15.6 24.5 %all_to_all.15.x_ref = f32[16,176,128]{2,1,0:T(8,128)S(1)} all-to-all(f32[16,176,128]{2,1,0:T(8,128)S(1)} %add.8), channel_id=1, replica_groups={{0,16,32,48,64,80,96,112,128,144,160,176,192,208,224,240},{8,24,40,56,7..., dimensions={0} | all-to-all | bytes 2883584 | tf_op jit(solution)/shard_map/all_to_all | solution.py:342
  40.1 0.1 sum_copies.2
  40.2 26.6 %all_to_all.16.x_ref = f32[8,176,128]{2,1,0:T(8,128)S(1)} all-to-all(f32[8,176,128]{2,1,0:T(8,128)S(1)} %sum_copies.2), channel_id=1, replica_groups=mesh['blk'=32,'inner'=8] {'inner'}, dimensions={0} | all-to-all | bytes 1441792 | tf_op jit(solution)/shard_map/all_to_all | solution.py:347
  66.8 0.1 sum_copies.3
  67.0 21.7 %all_to_all.17.half_ref = f32[16,176,128]{2,1,0:T(8,128)S(1)} all-to-all(f32[16,176,128]{2,1,0:T(8,128)S(1)} %sum_copies.3), channel_id=1, replica_groups={{0,16,32,48,64,80,96,112,128,144,160,176,192,208,224,240},{8,24,40,56,7..., dimensions={0} | all-to-all | bytes 2883584 | tf_op jit(solution)/shard_map/all_to_all | solution.py:342
  88.7 5.1 %collective-permute-start.1 = (f32[16,176,128]{2,1,0:T(8,128)S(1)}, f32[16,176,128]{2,1,0:T(8,128)S(1)}, u32[]{:S(2)}, u32[]{:S(2)}) collective-permute-start(f32[16,176,128]{2,1,0:T(8,128)S(1)} %all_to_all.17.half_ref), channel_id=1, source_target_pairs={{0,8},{8,0},{16,24},{24,16},{32,40},{40,32},{48,56},{56,48},{64,72... | collective-permute-start | bytes 4325384 | tf_op jit(solution)/shard_map/ppermute | solution.py:349
  93.8 2.8 %collective-permute-done.1.other_ref = f32[16,176,128]{2,1,0:T(8,128)S(1)} collective-permute-done((f32[16,176,128]{2,1,0:T(8,128)S(1)}, f32[16,176,128]{2,1,0:T(8,128)S(1)}, u32[]{:S(2)}, u32[]{:S(2)}) %collective-permute-start.1) | collective-permute-done | bytes 1441824 | tf_op jit(solution)/shard_map/ppermute | solution.py:349
  96.6 11.7 %back.1 = (f32[320,1536]{1,0:T(8,128)}, f32[320,2048]{1,0:T(8,128)}) custom-call(s32[1]{0:T(128)} %bitcast.core_ref, f32[16,176,128]{2,1,0:T(8,128)S(1)} %all_to_all.17.half_ref, f32[16,176,128]{2,1,0:T(8,128)S(1)} %collective-permute-done.1.other_ref, bf16[320,1536]{1,0:T(8,128)(2,1)S(1)} %get-tuple-element.8.high_ref.high_hbm, ...), custom_call_target="tpu_custom_call" | custom-call | flops 3000000000 | bytes 10000000 | tf_op jit(solution)/shard_map/back/pallas_call | solution.py:351
Async XLA Ops:
  0.6 1.3 %copy-start = (bf16[2048,320]{0,1:T(8,128)(2,1)S(1)}, bf16[2048,320]{0,1:T(8,128)(2,1)}, u32[]{:S(2)}) copy-start(bf16[2048,320]{0,1:T(8,128)(2,1)} %param.3) | copy-start | bytes 3932164
  9.3 6.2 %collective-permute-start = (f32[16,176,128]{2,1,0:T(8,128)S(1)}, f32[16,176,128]{2,1,0:T(8,128)S(1)}, u32[]{:S(2)}, u32[]{:S(2)}) collective-permute-start(f32[16,176,128]{2,1,0:T(8,128)S(1)} %get-tuple-element.10), channel_id=1, source_target_pairs={{0,8},{8,0},{16,24},{24,16},{32,40},{40,32},{48,56},{56,48},{64,72... | collective-permute-start | bytes 4325384 | tf_op jit(solution)/shard_map/ppermute | solution.py:345
  88.7 8.0 %collective-permute-start.1 = (f32[16,176,128]{2,1,0:T(8,128)S(1)}, f32[16,176,128]{2,1,0:T(8,128)S(1)}, u32[]{:S(2)}, u32[]{:S(2)}) collective-permute-start(f32[16,176,128]{2,1,0:T(8,128)S(1)} %all_to_all.17.half_ref), channel_id=1, source_target_pairs={{0,8},{8,0},{16,24},{24,16},{32,40},{40,32},{48,56},{56,48},{64,72... | collective-permute-start | bytes 4325384 | tf_op jit(solution)/shard_map/ppermute | solution.py:349

commit v5 on v4

--- a/solution.py
+++ b/solution.py
@@ -162,13 +162,14 @@
     gram = by_high[:, 0:tall] + (mixed + mixed.T + mxu(mid, mid, ROWS_OF))
     gram = gram * (1.0 / row_total)
     corner = jnp.concatenate([gram[256:320, 256:320], gram[64:128, 64:128]], axis=1)
-    zero = jnp.concatenate([gram[0:64, 0:128], corner, gram[0:128, 128:256]], axis=0)
+    both = jnp.concatenate([gram[0:64, 0:128], corner], axis=0).reshape(CHIPS, 8, LANES)
     last = jnp.concatenate([gram[0:128, 256:320], gram[128:256, 256:320]], axis=1)
-    one = jnp.concatenate([last, gram[128:256, 128:256]], axis=0)
-    own = jnp.where(core == 0, zero, one).reshape(CHIPS, 16, LANES)
-    far = jnp.where(core == 0, one, zero).reshape(CHIPS, 16, LANES)
-    own_ref[...] = own
-    give_ref[:, tall // 2 :, :] = far
+    zero = jnp.concatenate([gram[0:128, 128:256], last], axis=0).reshape(CHIPS, 16, LANES)
+    one = jnp.concatenate([gram[128:256, 128:256]] * 2, axis=0).reshape(CHIPS, 16, LANES)
+    own_ref[:, 0:8, :] = both
+    own_ref[:, 8:24, :] = jnp.where(core == 0, zero, one)
+    give_ref[:, tall // 2 : tall // 2 + 8, :] = both
+    give_ref[:, tall // 2 + 8 :, :] = jnp.where(core == 0, one, zero)
 
 
 def front(core, latents, test_t, row_total):
@@ -181,8 +182,8 @@
         [
             shape(tall, rows, dtype=bf16),
             shape(tall, rows, dtype=bf16),
-            shape(CHIPS, 16, LANES),
-            shape(CHIPS, tall // 2 + 16, LANES),
+            shape(CHIPS, 24, LANES),
+            shape(CHIPS, tall // 2 + 24, LANES),
         ],
         [SMEM, HBM, HBM],
         [VMEM] * 4,
@@ -219,7 +220,7 @@
     return call(
         keep_kernel,
         "keep",
-        shape(CHIPS, tall // 2 + 16, LANES),
+        shape(CHIPS, tall // 2 + 24, LANES),
         [SMEM, HBM, VMEM, VMEM],
         VMEM,
         [pltpu.VMEM((2, rows, width // 4), jnp.bfloat16), pltpu.SemaphoreType.DMA((2,))],
@@ -241,43 +242,69 @@
     return call(sum_copies_kernel, "sum_copies", shape(count, *x.shape[1:]), [VMEM], VMEM)(x)
 
 
+def first_kernel(half_ref, high_hbm, mid_hbm, m_ref, high, low, scratch, sems):
+    rows = high_hbm.shape[1]
+    edge = high.shape[0] // 2
+    loads = [
+        pltpu.make_async_copy(high_hbm, high.at[:, pl.ds(0, rows)], sems.at[0]),
+        pltpu.make_async_copy(mid_hbm, low.at[:, pl.ds(0, rows)], sems.at[1]),
+    ]
+    for load in loads:
+        load.start()
+    both = half_ref[:, edge : edge + 8, :].reshape(LANES, LANES)
+    left = jnp.concatenate([both[0:64, 64:128].T, both[64:128, 64:128]], axis=1)
+    m_ref[...] = factor_inverse(jnp.concatenate([both[0:64], left], axis=0), 128, scratch)
+    split_tiles(half_ref, high, low, rows)
+    for load in loads:
+        load.wait()
+
+
+def split_tiles(ref, high, low, first):
+    edge = high.shape[0] // 2
+    for j in range(CHIPS):
+        here = pl.ds(first + (j // 2) * LANES, LANES)
+        part = pl.ds((j % 2) * edge, edge)
+        high[part, here], low[part, here] = bf16_parts(ref[j, 0:edge, :])
+
+
 def back_kernel(
-    scale, core_ref, half_ref, other_ref, high_hbm, mid_hbm, basis_hbm, proj_hbm,
-    high, low, basis, proj, scratch, in_sems, basis_sems, proj_sems,
+    scale, core_ref, m_ref, high_ref, low_ref, half_ref, other_ref, basis_hbm, proj_hbm,
+    high, low, rest_high, rest_low, basis, proj, scratch, basis_sems, proj_sems,
 ):
     core = core_ref[0]
     tall, width = proj.shape
     rows = basis.shape[1]
     edge = tall // 2
-    loads = [
-        pltpu.make_async_copy(high_hbm, high.at[:, pl.ds(0, rows)], in_sems.at[0]),
-        pltpu.make_async_copy(mid_hbm, low.at[:, pl.ds(0, rows)], in_sems.at[1]),
-    ]
-    for load in loads:
-        load.start()
-    own = half_ref[:, edge:, :].reshape(256, LANES)
-    far = other_ref[:, edge:, :].reshape(256, LANES)
+    own = half_ref[:, edge + 8 :, :].reshape(256, LANES)
+    far = other_ref[:, edge + 8 :, :].reshape(256, LANES)
     zero = jnp.where(core == 0, own, far)
-    one = jnp.where(core == 0, far, own)
-    for side, ref in enumerate((half_ref, other_ref)):
-        for j in range(CHIPS):
-            here = pl.ds(rows + side * (width // 2) + (j // 2) * LANES, LANES)
-            part = pl.ds((j % 2) * edge, edge)
-            high[part, here], low[part, here] = bf16_parts(ref[j, 0:edge, :])
-
-    def product(first, m):
-        count, depth = m.shape
+    g11 = jnp.where(core == 0, far, own)[0:128]
+    split_tiles(other_ref, high, low, 0)
+
+    def columns(c, depth):
+        part = slice(512 * c, 512 * c + 512)
+        if part.stop <= rows + width // 2:
+            return high_ref[depth, part], low_ref[depth, part]
+        there = slice(part.start - rows - width // 2, part.stop - rows - width // 2)
+        return high[depth, there], low[depth, there]
+
+    def store(first, c, y):
+        at = 512 * c
+        if at < rows:
+            basis[first : first + y.shape[0], at : at + 512] = y
+        else:
+            proj[first : first + y.shape[0], at - rows : at - rows + 512] = y * scale
+
+    def times(m, x):
+        both, m_high = m
+        by_high = mxu(both, x[0])
+        return by_high[: m_high.shape[0]] + (mxu(m_high, x[1]) + by_high[m_high.shape[0] :])
+
+    def stacked(m):
         m_high, m_low = bf16_parts(m)
-        m_both = jnp.concatenate([m_high, m_low], axis=0)
-        for c in range((rows + width) // 512):
-            part = slice(512 * c, 512 * c + 512)
-            x_high, x_low = high[0:depth, part], low[0:depth, part]
-            by_high = mxu(m_both, x_high)
-            y = by_high[:count] + (mxu(m_high, x_low) + by_high[count:])
-            if 512 * c < rows:
-                basis[first : first + count, part] = y
-            else:
-                proj[first : first + count, 512 * c - rows : 512 * c + 512 - rows] = y * scale
+        return jnp.concatenate([m_high, m_low], axis=0), m_high
+
+    steps = (rows + width) // 512
 
     copies = []
 
@@ -298,18 +325,17 @@
         for copy in copies[-3:]:
             copy.start()
 
-    left = jnp.concatenate([zero[0:64, 64:128].T, zero[64:128, 64:128]], axis=1)
-    g00 = jnp.concatenate([zero[0:64], left], axis=0)
     blank = jnp.zeros((128, 64), jnp.float32)
-    g01 = jnp.concatenate([zero[128:256], one[0:128, 0:64], blank], axis=1)
-    g12 = jnp.concatenate([one[0:128, 64:128], blank], axis=1)
-    g22 = jnp.concatenate([zero[64:128, 0:64], blank[0:64]], axis=1)
-    m0 = factor_inverse(g00, 128, scratch)
-    for load in loads:
-        load.wait()
+    g01 = jnp.concatenate([zero[0:128], zero[128:256, 0:64], blank], axis=1)
+    g12 = jnp.concatenate([zero[128:256, 64:128], blank], axis=1)
+    corner = half_ref[CHIPS // 2 :, edge : edge + 8, :].reshape(64, LANES)
+    g22 = jnp.concatenate([corner[:, 0:64], blank[0:64]], axis=1)
+    m0 = m_ref[...]
     a01 = dot(m0, g01)
-    s11 = one[128:256] - dot_t(a01[:, 0:128], a01[:, 0:128])
-    product(0, m0)
+    s11 = g11 - dot_t(a01[:, 0:128], a01[:, 0:128])
+    left = stacked(m0)
+    for c in range(steps):
+        store(0, c, times(left, columns(c, slice(0, 128))))
     m1 = factor_inverse(s11, 128, scratch)
     s12 = g12 - dot_t(a01[:, 0:128], a01[:, 128:256])
     s22 = g22 - dot_t(a01[:, 128:256], a01[:, 128:256])[0:64]
@@ -318,13 +344,24 @@
     a12 = dot(m1, s12)
     s22 = s22 - dot_t(a12, a12)[0:64]
     b10 = dot(m1, b0[0:128])
-    product(128, jnp.concatenate([b10, m1], axis=1))
-    m2 = factor_inverse(s22, 64, scratch)
     b20 = b0[128:192] - dot_t(a12, b10)[0:64]
     b21 = -dot_t(a12, m1)[0:64]
+    top = jnp.concatenate([b10, m1], axis=1)
+    left = stacked(jnp.concatenate([top, jnp.concatenate([b20, b21], axis=1)], axis=0))
+    for c in range(steps):
+        y = times(left, columns(c, slice(0, 256)))
+        store(128, c, y[0:128])
+        x_high, x_low = columns(c, slice(256, 320))
+        rest = y[128:192] + (x_high.astype(jnp.float32) + x_low.astype(jnp.float32))
+        rest_high[:, 512 * c : 512 * c + 512], rest_low[:, 512 * c : 512 * c + 512] = bf16_parts(
+            rest
+        )
+    m2 = factor_inverse(s22, 64, scratch)
     send(1, 128, 128)
-    m2 = m2[:, 0:64]
-    product(256, jnp.concatenate([dot(m2, b20), dot(m2, b21), m2], axis=1))
+    left = stacked(m2[:, 0:64])
+    for c in range(steps):
+        part = slice(512 * c, 512 * c + 512)
+        store(256, c, times(left, (rest_high[:, part], rest_low[:, part])))
     send(2, 256, 64)
     for copy in copies:
         copy.wait()
@@ -348,25 +385,36 @@
     half = over_chips(sum_copies(chunk, CHIPS))
     other = lax.ppermute(half, "blk", swap)
     bf16 = jnp.bfloat16
+    ready = rows + width // 2
+    inverse, high, low = call(
+        first_kernel,
+        "first",
+        [shape(LANES, LANES)] + [shape(tall, ready, dtype=bf16)] * 2,
+        [VMEM, HBM, HBM],
+        [VMEM] * 3,
+        [pltpu.VMEM((9 * LANES, LANES), jnp.float32), pltpu.SemaphoreType.DMA((2,))],
+        flops=4 * 10**9,
+    )(half, high, mid)
     basis_t, projection = call(
         functools.partial(back_kernel, float(width) ** 0.5 / row_total),
         "back",
         [shape(tall, rows), shape(tall, width)],
-        [SMEM, VMEM, VMEM, HBM, HBM],
+        [SMEM] + [VMEM] * 5,
         [HBM, HBM],
         [
-            pltpu.VMEM((tall, rows + width), bf16),
-            pltpu.VMEM((tall, rows + width), bf16),
+            pltpu.VMEM((tall, width // 2), bf16),
+            pltpu.VMEM((tall, width // 2), bf16),
+            pltpu.VMEM((64, rows + width), bf16),
+            pltpu.VMEM((64, rows + width), bf16),
             pltpu.VMEM((tall, rows), jnp.float32),
             pltpu.VMEM((tall, width), jnp.float32),
             pltpu.VMEM((9 * LANES, LANES), jnp.float32),
-            pltpu.SemaphoreType.DMA((2,)),
             pltpu.SemaphoreType.DMA((3,)),
             pltpu.SemaphoreType.DMA((3, 2)),
         ],
         flops=3 * 10**9,
         moved=10**7,
-    )(core, half, other, high, mid)
+    )(core, inverse, high, low, half, other)
     return (basis_t.T, projection)
 
 

time: 109 us -> 107 us (0.982)
  blocking collectives: 72.8 us -> 75.6 us
  waiting for transfers between devices: 2.92 us -> 0.16 us
    pallas_call x1, Pallas kernels: 11.7 us -> 7.41 us  [shards(): call(functools.partial(back_kernel, float(width) ** 0.5 / row_total), 'ba...]
    pallas_call x1 -> x2, Pallas kernels: 2.77 us -> 6.39 us  [the longest x1 3.62 us: shards(): call(first_kernel, 'first', [shape(LANES, LANES)] + [shape(tall, ready, d...]
    ppermute x1, waiting for transfers between devices: 2.85 us -> 0.01 us  [shards(): other = lax.ppermute(half, 'blk', swap)]
    all_to_all x2, blocking collectives: 46.2 us -> 48 us  [over_chips(): return lax.all_to_all(value, 'blk', 0, 0, axis_index_groups=groups)]
  transfers between devices with their start and end apart: 2 -> 2, of which waited for: 2 -> 1; matrix products, arithmetic and copies ran while one was open for 0% -> 0% of each run, Pallas kernels for 3% -> 6%
where the time goes in v5:
time: 107 us
  blocking collectives  75.6 us (71%)
  Pallas kernels  21.3 us (20%)
  starting transfers between devices  7.76 us (7%)
  local copies, waits for them, and re-layouts  1.31 us (1%)
    all_to_all x2, blocking collectives, over_chips(): return lax.all_to_all(value, 'blk', 0, 0, axis_index_groups=groups)  48 us
    all_to_all x1, blocking collectives, shards(): chunk = lax.all_to_all(sum_copies(chunks, DEPTH), 'inner', 0, 0)  27.6 us
    pallas_call x1, Pallas kernels, shards(): call(functools.partial(back_kernel, float(width) ** 0.5 / row_total), 'ba...  7.41 us
    pallas_call x1, Pallas kernels, front(): call(functools.partial(front_kernel, row_total), 'front', [shape(tall, ro...  7.33 us
    ppermute x1, starting transfers between devices, shards(): other = lax.ppermute(half, 'blk', swap)  4.42 us
    pallas_call x1, Pallas kernels, shards(): call(first_kernel, 'first', [shape(LANES, LANES)] + [shape(tall, ready, d...  3.62 us
    ppermute x1, starting transfers between devices, shards(): given = lax.ppermute(give, 'blk', swap)  3.33 us
    pallas_call x1, Pallas kernels, keep_half(): call(keep_kernel, 'keep', shape(CHIPS, tall // 2 + 24, LANES), [SMEM, HBM...  2.77 us
  transfers between devices with their start and end apart: 2, of which 1 were waited for; matrix products, arithmetic and copies ran while one was open for 0% of the time, Pallas kernels for 6%

profile of v5, /device:TPU:1, one launch (start us, length us, event | category | flops | bytes accessed | tf_op | source)
XLA Modules:
  0.0 107.2 jit_solution(1941653968588615937)
XLA Ops:
  0.6 0.0 copy-start
  0.7 1.3 %copy-done = bf16[2048,320]{0,1:T(8,128)(2,1)S(1)} copy-done((bf16[2048,320]{0,1:T(8,128)(2,1)S(1)}, bf16[2048,320]{0,1:T(8,128)(2,1)}, u32[]{:S(2)}) %copy-start) | copy-done | bytes 1310744
  2.0 7.3 %front.1 = (bf16[320,1536]{1,0:T(8,128)(2,1)S(1)}, bf16[320,1536]{1,0:T(8,128)(2,1)S(1)}, f32[16,24,128]{2,1,0:T(8,128)S(1)}, f32[16,184,128]{2,1,0:T(8,128)S(1)}) custom-call(s32[1]{0:T(128)} %bitcast.core_ref, bf16[1536,2048]{1,0:T(8,128)(2,1)} %lat_hbm.3, bf16[320,2048]{1,0:T(8,128)(2,1)S(1)} %bitcast.3), custom_call_target="tpu_custom_call" | custom-call | flops 6000000000 | bytes 10000000 | tf_op jit(solution)/shard_map/front/pallas_call | solution.py:179
  9.3 3.3 %collective-permute-start = (f32[16,184,128]{2,1,0:T(8,128)S(1)}, f32[16,184,128]{2,1,0:T(8,128)S(1)}, u32[]{:S(2)}, u32[]{:S(2)}) collective-permute-start(f32[16,184,128]{2,1,0:T(8,128)S(1)} %get-tuple-element.13), channel_id=1, source_target_pairs={{0,8},{8,0},{16,24},{24,16},{32,40},{40,32},{48,56},{56,48},{64,72... | collective-permute-start | bytes 4521992 | tf_op jit(solution)/shard_map/ppermute | solution.py:382
  12.6 2.8 %keep.1 = f32[16,184,128]{2,1,0:T(8,128)S(1)} custom-call(s32[1]{0:T(128)} %bitcast.core_ref, bf16[1536,2048]{1,0:T(8,128)(2,1)} %lat_hbm.3, bf16[320,1536]{1,0:T(8,128)(2,1)S(1)} %get-tuple-element.11.high_ref.high_hbm, f32[16,24,128]{2,1,0:T(8,128)S(1)} %get-tuple-element.12.own_ref), custom_call_target="tpu_custom_call" | custom-call | flops 1000000000 | bytes 5000000 | tf_op jit(solution)/shard_map/keep/pallas_call | solution.py:220
  15.4 0.2 collective-permute-done
  15.6 0.2 add.8
  15.7 25.8 %all_to_all.15.x_ref = f32[16,184,128]{2,1,0:T(8,128)S(1)} all-to-all(f32[16,184,128]{2,1,0:T(8,128)S(1)} %add.8), channel_id=1, replica_groups={{0,16,32,48,64,80,96,112,128,144,160,176,192,208,224,240},{8,24,40,56,7..., dimensions={0} | all-to-all | bytes 3014656 | tf_op jit(solution)/shard_map/all_to_all | solution.py:379
  41.5 0.1 sum_copies.2
  41.6 27.6 %all_to_all.16.x_ref = f32[8,184,128]{2,1,0:T(8,128)S(1)} all-to-all(f32[8,184,128]{2,1,0:T(8,128)S(1)} %sum_copies.2), channel_id=1, replica_groups=mesh['blk'=32,'inner'=8] {'inner'}, dimensions={0} | all-to-all | bytes 1507328 | tf_op jit(solution)/shard_map/all_to_all | solution.py:384
  69.2 0.1 sum_copies.3
  69.3 22.2 %all_to_all.17.half_ref = f32[16,184,128]{2,1,0:T(8,128)S(1)} all-to-all(f32[16,184,128]{2,1,0:T(8,128)S(1)} %sum_copies.3), channel_id=1, replica_groups={{0,16,32,48,64,80,96,112,128,144,160,176,192,208,224,240},{8,24,40,56,7..., dimensions={0} | all-to-all | bytes 3014656 | tf_op jit(solution)/shard_map/all_to_all | solution.py:379
  91.5 4.4 %collective-permute-start.1 = (f32[16,184,128]{2,1,0:T(8,128)S(1)}, f32[16,184,128]{2,1,0:T(8,128)S(1)}, u32[]{:S(2)}, u32[]{:S(2)}) collective-permute-start(f32[16,184,128]{2,1,0:T(8,128)S(1)} %all_to_all.17.half_ref), channel_id=1, source_target_pairs={{0,8},{8,0},{16,24},{24,16},{32,40},{40,32},{48,56},{56,48},{64,72... | collective-permute-start | bytes 4521992 | tf_op jit(solution)/shard_map/ppermute | solution.py:386
  96.0 3.6 %first.1 = (f32[128,128]{1,0:T(8,128)S(1)}, bf16[320,2560]{1,0:T(8,128)(2,1)S(1)}, bf16[320,2560]{1,0:T(8,128)(2,1)S(1)}) custom-call(f32[16,184,128]{2,1,0:T(8,128)S(1)} %all_to_all.17.half_ref, bf16[320,1536]{1,0:T(8,128)(2,1)S(1)} %get-tuple-element.11.high_ref.high_hbm, bf16[320,1536]{1,0:T(8,128)(2,1)S(1)} %get-tuple-element.14.mid_hbm), custom_call_target="tpu_custom_call" | custom-call | flops 4000000000 | bytes 1000000 | tf_op jit(solution)/shard_map/first/pallas_call | solution.py:389
  99.6 0.0 collective-permute-done.1.other_ref
  99.6 7.4 %back.1 = (f32[320,1536]{1,0:T(8,128)}, f32[320,2048]{1,0:T(8,128)}) custom-call(s32[1]{0:T(128)} %bitcast.core_ref, f32[128,128]{1,0:T(8,128)S(1)} %get-tuple-element.15.m_ref, bf16[320,2560]{1,0:T(8,128)(2,1)S(1)} %get-tuple-element.16.high_ref, bf16[320,2560]{1,0:T(8,128)(2,1)S(1)} %get-tuple-element.17.low_ref, f32[16,184,128]{2,1,0:T(8,128)S(1)} %all_to_all.17.half_ref, ...), custom_call_target="tpu_custom_call" | custom-call | flops 3000000000 | bytes 10000000 | tf_op jit(solution)/shard_map/back/pallas_call | solution.py:398
Async XLA Ops:
  0.6 1.3 %copy-start = (bf16[2048,320]{0,1:T(8,128)(2,1)S(1)}, bf16[2048,320]{0,1:T(8,128)(2,1)}, u32[]{:S(2)}) copy-start(bf16[2048,320]{0,1:T(8,128)(2,1)} %param.3) | copy-start | bytes 3932164
  9.3 6.3 %collective-permute-start = (f32[16,184,128]{2,1,0:T(8,128)S(1)}, f32[16,184,128]{2,1,0:T(8,128)S(1)}, u32[]{:S(2)}, u32[]{:S(2)}) collective-permute-start(f32[16,184,128]{2,1,0:T(8,128)S(1)} %get-tuple-element.13), channel_id=1, source_target_pairs={{0,8},{8,0},{16,24},{24,16},{32,40},{40,32},{48,56},{56,48},{64,72... | collective-permute-start | bytes 4521992 | tf_op jit(solution)/shard_map/ppermute | solution.py:382
  91.5 8.1 %collective-permute-start.1 = (f32[16,184,128]{2,1,0:T(8,128)S(1)}, f32[16,184,128]{2,1,0:T(8,128)S(1)}, u32[]{:S(2)}, u32[]{:S(2)}) collective-permute-start(f32[16,184,128]{2,1,0:T(8,128)S(1)} %all_to_all.17.half_ref), channel_id=1, source_target_pairs={{0,8},{8,0},{16,24},{24,16},{32,40},{40,32},{48,56},{56,48},{64,72... | collective-permute-start | bytes 4521992 | tf_op jit(solution)/shard_map/ppermute | solution.py:386

commit v6 on v5

--- a/solution.py
+++ b/solution.py
@@ -29,6 +29,13 @@
     sub = lax.broadcasted_iota(jnp.int32, (8, LANES), 0)
     pivots = []
 
+    on_diagonal = [jnp.where(lane == sub + 8 * t, tiles[t], 0.0) for t in range(count)]
+    by_lane = lax.rsqrt(jnp.sum(sum(on_diagonal), axis=0, keepdims=True))
+    by_lane = jnp.where(lane < n, jnp.broadcast_to(by_lane, (8, LANES)), 1.0)
+    for t in range(count):
+        by_row = lax.rsqrt(jnp.sum(on_diagonal[t], axis=1, keepdims=True))
+        tiles[t] = tiles[t] * by_lane * by_row
+
     def over_lanes(x, j):
         return jnp.broadcast_to(x[:, j : j + 1], (8, LANES))
 
@@ -46,20 +53,30 @@
         square = [[row(8 * k + m) for k in range(m + 1)] for m in range(STEP)]
         rows = [row(64 + m) for m in range(STEP)]
         lower = [[None] * STEP for _ in range(STEP)]
-        inverse = []
+        inverse = [None] * STEP
         pivot = square[0][0]
-        for k in range(STEP):
-            if k:
-                pivot = jnp.where(sub == k, square[k][k], pivot)
-            inverse.append(1.0 / square[k][k])
-            for m in range(k + 1, STEP):
+        for k in range(0, STEP, 2):
+            a, b, c = square[k][k], square[k + 1][k], square[k + 1][k + 1]
+            determinant = a * c - b * b
+            inverse[k] = 1.0 / a
+            inverse[k + 1] = a * (1.0 / determinant)
+            pivot = jnp.where(sub == k, a, pivot)
+            pivot = jnp.where(sub == k + 1, determinant * inverse[k], pivot)
+            lower[k + 1][k] = b * inverse[k]
+            second = [None] * STEP
+            for m in range(k + 2, STEP):
                 lower[m][k] = square[m][k] * inverse[k]
-            for m in range(k + 1, STEP):
+                second[m] = square[m][k + 1] - square[m][k] * lower[k + 1][k]
+                lower[m][k + 1] = second[m] * inverse[k + 1]
+            for m in range(k + 2, STEP):
                 for i in range(m, STEP):
-                    square[i][m] = square[i][m] - square[i][k] * lower[m][k]
-            rows[k] = jnp.where(lane == j + k, 1.0, rows[k])
-            for m in range(k + 1, STEP):
-                rows[m] = rows[m] - lower[m][k] * rows[k]
+                    square[i][m] = (
+                        square[i][m] - square[i][k] * lower[m][k] - second[i] * lower[m][k + 1]
+                    )
+            for q in (k, k + 1):
+                rows[q] = jnp.where(lane == j + q, 1.0, rows[q])
+                for m in range(q + 1, STEP):
+                    rows[m] = rows[m] - lower[m][q] * rows[q]
         pivots.append(pivot)
         done = rows[0]
         for k in range(1, STEP):
@@ -76,7 +93,7 @@
             tiles[t] = x
     out = []
     for t in range(count):
-        out.append(jnp.where(lane <= sub + 8 * t, tiles[t] * lax.rsqrt(pivots[t]), 0.0))
+        out.append(jnp.where(lane <= sub + 8 * t, tiles[t] * lax.rsqrt(pivots[t]) * by_lane, 0.0))
     return jnp.concatenate(out, axis=0)
 
 
@@ -279,7 +296,6 @@
     far = other_ref[:, edge + 8 :, :].reshape(256, LANES)
     zero = jnp.where(core == 0, own, far)
     g11 = jnp.where(core == 0, far, own)[0:128]
-    split_tiles(other_ref, high, low, 0)
 
     def columns(c, depth):
         part = slice(512 * c, 512 * c + 512)
@@ -333,6 +349,7 @@
     m0 = m_ref[...]
     a01 = dot(m0, g01)
     s11 = g11 - dot_t(a01[:, 0:128], a01[:, 0:128])
+    split_tiles(other_ref, high, low, 0)
     left = stacked(m0)
     for c in range(steps):
         store(0, c, times(left, columns(c, slice(0, 128))))

time: 107 us -> 107 us (level)
  no operation moved by 1% of the time
where the time goes in v6:
time: 107 us
  blocking collectives  75.6 us (71%)
  Pallas kernels  20.9 us (20%)
  starting transfers between devices  7.76 us (7%)
  local copies, waits for them, and re-layouts  1.31 us (1%)
    all_to_all x2, blocking collectives, over_chips(): return lax.all_to_all(value, 'blk', 0, 0, axis_index_groups=groups)  48 us
    all_to_all x1, blocking collectives, shards(): chunk = lax.all_to_all(sum_copies(chunks, DEPTH), 'inner', 0, 0)  27.6 us
    pallas_call x1, Pallas kernels, front(): call(functools.partial(front_kernel, row_total), 'front', [shape(tall, ro...  7.33 us
    pallas_call x1, Pallas kernels, shards(): call(functools.partial(back_kernel, float(width) ** 0.5 / row_total), 'ba...  7.3 us
    ppermute x1, starting transfers between devices, shards(): other = lax.ppermute(half, 'blk', swap)  4.42 us
    ppermute x1, starting transfers between devices, shards(): given = lax.ppermute(give, 'blk', swap)  3.33 us
    pallas_call x1, Pallas kernels, shards(): call(first_kernel, 'first', [shape(LANES, LANES)] + [shape(tall, ready, d...  3.29 us
    pallas_call x1, Pallas kernels, keep_half(): call(keep_kernel, 'keep', shape(CHIPS, tall // 2 + 24, LANES), [SMEM, HBM...  2.77 us
  transfers between devices with their start and end apart: 2, of which 1 were waited for; matrix products, arithmetic and copies ran while one was open for 0% of the time, Pallas kernels for 6%

profile of v6, /device:TPU:1, one launch (start us, length us, event | category | flops | bytes accessed | tf_op | source)
XLA Modules:
  0.0 106.7 jit_solution(5547150628653366)
XLA Ops:
  0.6 0.0 copy-start
  0.7 1.3 %copy-done = bf16[2048,320]{0,1:T(8,128)(2,1)S(1)} copy-done((bf16[2048,320]{0,1:T(8,128)(2,1)S(1)}, bf16[2048,320]{0,1:T(8,128)(2,1)}, u32[]{:S(2)}) %copy-start) | copy-done | bytes 1310744
  2.0 7.3 %front.1 = (bf16[320,1536]{1,0:T(8,128)(2,1)S(1)}, bf16[320,1536]{1,0:T(8,128)(2,1)S(1)}, f32[16,24,128]{2,1,0:T(8,128)S(1)}, f32[16,184,128]{2,1,0:T(8,128)S(1)}) custom-call(s32[1]{0:T(128)} %bitcast.core_ref, bf16[1536,2048]{1,0:T(8,128)(2,1)} %lat_hbm.3, bf16[320,2048]{1,0:T(8,128)(2,1)S(1)} %bitcast.3), custom_call_target="tpu_custom_call" | custom-call | flops 6000000000 | bytes 10000000 | tf_op jit(solution)/shard_map/front/pallas_call | solution.py:196
  9.3 3.3 %collective-permute-start = (f32[16,184,128]{2,1,0:T(8,128)S(1)}, f32[16,184,128]{2,1,0:T(8,128)S(1)}, u32[]{:S(2)}, u32[]{:S(2)}) collective-permute-start(f32[16,184,128]{2,1,0:T(8,128)S(1)} %get-tuple-element.13), channel_id=1, source_target_pairs={{0,8},{8,0},{16,24},{24,16},{32,40},{40,32},{48,56},{56,48},{64,72... | collective-permute-start | bytes 4521992 | tf_op jit(solution)/shard_map/ppermute | solution.py:399
  12.6 2.8 %keep.1 = f32[16,184,128]{2,1,0:T(8,128)S(1)} custom-call(s32[1]{0:T(128)} %bitcast.core_ref, bf16[1536,2048]{1,0:T(8,128)(2,1)} %lat_hbm.3, bf16[320,1536]{1,0:T(8,128)(2,1)S(1)} %get-tuple-element.11.high_ref.high_hbm, f32[16,24,128]{2,1,0:T(8,128)S(1)} %get-tuple-element.12.own_ref), custom_call_target="tpu_custom_call" | custom-call | flops 1000000000 | bytes 5000000 | tf_op jit(solution)/shard_map/keep/pallas_call | solution.py:237
  15.4 0.2 collective-permute-done
  15.6 0.2 add.8
  15.7 25.8 %all_to_all.15.x_ref = f32[16,184,128]{2,1,0:T(8,128)S(1)} all-to-all(f32[16,184,128]{2,1,0:T(8,128)S(1)} %add.8), channel_id=1, replica_groups={{0,16,32,48,64,80,96,112,128,144,160,176,192,208,224,240},{8,24,40,56,7..., dimensions={0} | all-to-all | bytes 3014656 | tf_op jit(solution)/shard_map/all_to_all | solution.py:396
  41.5 0.1 sum_copies.2
  41.6 27.6 %all_to_all.16.x_ref = f32[8,184,128]{2,1,0:T(8,128)S(1)} all-to-all(f32[8,184,128]{2,1,0:T(8,128)S(1)} %sum_copies.2), channel_id=1, replica_groups=mesh['blk'=32,'inner'=8] {'inner'}, dimensions={0} | all-to-all | bytes 1507328 | tf_op jit(solution)/shard_map/all_to_all | solution.py:401
  69.2 0.1 sum_copies.3
  69.3 22.2 %all_to_all.17.half_ref = f32[16,184,128]{2,1,0:T(8,128)S(1)} all-to-all(f32[16,184,128]{2,1,0:T(8,128)S(1)} %sum_copies.3), channel_id=1, replica_groups={{0,16,32,48,64,80,96,112,128,144,160,176,192,208,224,240},{8,24,40,56,7..., dimensions={0} | all-to-all | bytes 3014656 | tf_op jit(solution)/shard_map/all_to_all | solution.py:396
  91.5 4.4 %collective-permute-start.1 = (f32[16,184,128]{2,1,0:T(8,128)S(1)}, f32[16,184,128]{2,1,0:T(8,128)S(1)}, u32[]{:S(2)}, u32[]{:S(2)}) collective-permute-start(f32[16,184,128]{2,1,0:T(8,128)S(1)} %all_to_all.17.half_ref), channel_id=1, source_target_pairs={{0,8},{8,0},{16,24},{24,16},{32,40},{40,32},{48,56},{56,48},{64,72... | collective-permute-start | bytes 4521992 | tf_op jit(solution)/shard_map/ppermute | solution.py:403
  96.0 3.3 %first.1 = (f32[128,128]{1,0:T(8,128)S(1)}, bf16[320,2560]{1,0:T(8,128)(2,1)S(1)}, bf16[320,2560]{1,0:T(8,128)(2,1)S(1)}) custom-call(f32[16,184,128]{2,1,0:T(8,128)S(1)} %all_to_all.17.half_ref, bf16[320,1536]{1,0:T(8,128)(2,1)S(1)} %get-tuple-element.11.high_ref.high_hbm, bf16[320,1536]{1,0:T(8,128)(2,1)S(1)} %get-tuple-element.14.mid_hbm), custom_call_target="tpu_custom_call" | custom-call | flops 4000000000 | bytes 1000000 | tf_op jit(solution)/shard_map/first/pallas_call | solution.py:406
  99.3 0.0 collective-permute-done.1.other_ref
  99.3 7.3 %back.1 = (f32[320,1536]{1,0:T(8,128)}, f32[320,2048]{1,0:T(8,128)}) custom-call(s32[1]{0:T(128)} %bitcast.core_ref, f32[128,128]{1,0:T(8,128)S(1)} %get-tuple-element.15.m_ref, bf16[320,2560]{1,0:T(8,128)(2,1)S(1)} %get-tuple-element.16.high_ref, bf16[320,2560]{1,0:T(8,128)(2,1)S(1)} %get-tuple-element.17.low_ref, f32[16,184,128]{2,1,0:T(8,128)S(1)} %all_to_all.17.half_ref, ...), custom_call_target="tpu_custom_call" | custom-call | flops 3000000000 | bytes 10000000 | tf_op jit(solution)/shard_map/back/pallas_call | solution.py:415
Async XLA Ops:
  0.6 1.3 %copy-start = (bf16[2048,320]{0,1:T(8,128)(2,1)S(1)}, bf16[2048,320]{0,1:T(8,128)(2,1)}, u32[]{:S(2)}) copy-start(bf16[2048,320]{0,1:T(8,128)(2,1)} %param.3) | copy-start | bytes 3932164
  9.3 6.3 %collective-permute-start = (f32[16,184,128]{2,1,0:T(8,128)S(1)}, f32[16,184,128]{2,1,0:T(8,128)S(1)}, u32[]{:S(2)}, u32[]{:S(2)}) collective-permute-start(f32[16,184,128]{2,1,0:T(8,128)S(1)} %get-tuple-element.13), channel_id=1, source_target_pairs={{0,8},{8,0},{16,24},{24,16},{32,40},{40,32},{48,56},{56,48},{64,72... | collective-permute-start | bytes 4521992 | tf_op jit(solution)/shard_map/ppermute | solution.py:399
  91.5 7.7 %collective-permute-start.1 = (f32[16,184,128]{2,1,0:T(8,128)S(1)}, f32[16,184,128]{2,1,0:T(8,128)S(1)}, u32[]{:S(2)}, u32[]{:S(2)}) collective-permute-start(f32[16,184,128]{2,1,0:T(8,128)S(1)} %all_to_all.17.half_ref), channel_id=1, source_target_pairs={{0,8},{8,0},{16,24},{24,16},{32,40},{40,32},{48,56},{56,48},{64,72... | collective-permute-start | bytes 4521992 | tf_op jit(solution)/shard_map/ppermute | solution.py:403
